TPU v7x, 32 devices: a whole 2x2x4 slice. The times are simulated.
32 devices in a mesh: seq: 4 (over y, x), chan: 8 (over z, core).
Axes of the slice: x: 2, y: 2, z: 4, core: 2. Of those that a mesh axis runs over, the one named last changes fastest.
Arguments:
- tokens_in: float32 [32768, 1024], P(('seq', 'chan')), may hold values from -6 to 6
- ln_gain: bfloat16 [2, 2, 1024], P(None, None, 'chan'), may hold values from 0.5 to 1.5
- ln_bias: bfloat16 [2, 2, 1024], P(None, None, 'chan'), may hold values from -3 to 3
- in_weight: bfloat16 [2, 1024, 3072], P(None, 'chan'), may hold values from -0.1875 to 0.1875
- short_weight: float32 [2, 3, 3, 1024], P(None, None, None, 'chan'), may hold values from -3 to 3
- filter_first: float32 [2, 33, 64], replicated, may hold values from -2 to 2
- filter_mid: float32 [2, 64, 64], replicated, may hold values from -1.5 to 1.5
- filter_last: float32 [2, 64, 1024], P(None, None, 'chan'), may hold values from -0.015625 to 0.015625
- conv_bias: float32 [2, 1024], P(None, 'chan'), may hold values from -4 to 4
- out_weight: bfloat16 [2, 1024, 1024], P(None, 'chan'), may hold values from -0.1875 to 0.1875
- up_weight: bfloat16 [2, 1024, 4096], P(None, 'chan'), may hold values from -0.1875 to 0.1875
- down_weight: bfloat16 [2, 4096, 1024], P(None, 'chan'), may hold values from -0.09375 to 0.09375
- group_kind: int32 [8], replicated, may hold values from 0 to 1, as said below
- filt_len: int32 [8], replicated, may hold values from 1024 to 4096, as said below
- decay_win: int32 [8], replicated, may hold values from 256 to 2048, as said below
- cotangent: float32 [32768, 1024], P(('seq', 'chan')), may hold values from -6 to 6
Outputs:
- tokens_out: float32 [32768, 1024], P(('seq', 'chan'))
- grad_tokens: float32 [32768, 1024], P(('seq', 'chan'))
- grad_ln_gain: float32 [2, 2, 1024], P(None, None, 'chan')
- grad_ln_bias: float32 [2, 2, 1024], P(None, None, 'chan')
- grad_in_weight: float32 [2, 1024, 3072], P(None, 'chan')
- grad_short_weight: float32 [2, 3, 3, 1024], P(None, None, None, 'chan')
- grad_filter_first: float32 [2, 33, 64], replicated
- grad_filter_mid: float32 [2, 64, 64], replicated
- grad_filter_last: float32 [2, 64, 1024], P(None, None, 'chan')
- grad_conv_bias: float32 [2, 1024], P(None, 'chan')
- grad_out_weight: float32 [2, 1024, 1024], P(None, 'chan')
- grad_up_weight: float32 [2, 1024, 4096], P(None, 'chan')
- grad_down_weight: float32 [2, 4096, 1024], P(None, 'chan')
Inputs may be any that keep to these rules, and one draw needn't show every extreme that they name: `group_kind`: exactly 4 groups are 1; groups 2 m and 2 m + 1 are alike. `filt_len`: at least 2048 where group_kind is 1, at most 2048 where it is 0. `decay_win`: from 512 where group_kind is 1, at most 1024 where it is 0.
All inputs are finite; a program needn't handle non-finite values.
Results may differ from a plain program's by a relative error of at most 0.023.
Values may be sent and summed in bfloat16 or wider, within the bound.
A program may use at most 1 GiB of HBM per device.

v0:
```python
import math

import jax
import jax.numpy as jnp
from jax import lax
from jax.sharding import PartitionSpec as P

LAYERS = 2
SHORT = 2048


HIGHEST = lax.Precision.HIGHEST


def precise_dot(left, right):
    return jnp.dot(left, right, precision=HIGHEST, preferred_element_type=jnp.float32)


def dot_lead(left, right):
    return lax.dot_general(
        left, right, (((0,), (0,)), ((), ())), preferred_element_type=jnp.float32
    )


def dot_trail(left, right):
    return lax.dot_general(
        left, right, (((1,), (1,)), ((), ())), preferred_element_type=jnp.float32
    )


def dot_cross(left, right):
    return lax.dot_general(
        left, right, (((0,), (1,)), ((), ())), preferred_element_type=jnp.float32
    )


def layer_norm(values, norm_gain, norm_bias):
    average = jnp.mean(values, axis=-1, keepdims=True)
    centred = values - average
    variance = jnp.mean(centred * centred, axis=-1, keepdims=True)
    return centred * lax.rsqrt(variance + 1e-05) * norm_gain + norm_bias


def position_features(positions, length):
    fraction = positions / length
    frequency = jnp.arange(1, 17, dtype=jnp.float32)
    angles = 2.0 * jnp.pi * fraction[:, None] * frequency[None, :]
    return jnp.concatenate([fraction[:, None], jnp.cos(angles), jnp.sin(angles)], axis=1)


def filter_columns(features, first_layer, middle, last_layer):
    hidden = jnp.sin(precise_dot(features, first_layer))
    hidden = jnp.sin(precise_dot(hidden, middle))
    return lax.dot_general(
        last_layer,
        hidden,
        (((0,), (1,)), ((), ())),
        precision=HIGHEST,
        preferred_element_type=jnp.float32,
    )


def angle_table(row_count, col_count, modulus):
    product = (
        jnp.arange(row_count, dtype=jnp.int32)[:, None]
        * jnp.arange(col_count, dtype=jnp.int32)[None, :]
        % modulus
    )
    angles = product.astype(jnp.float32) * (2.0 * math.pi / modulus)
    return (jnp.cos(angles), jnp.sin(angles))


def forward_dft(signal):
    length = signal.shape[-1]
    inner_size = 128
    outer_size = length // inner_size
    shaped = signal.reshape(signal.shape[:-1] + (outer_size, inner_size))
    cos_outer, sin_outer = angle_table(outer_size, outer_size, outer_size)
    cos_twist, sin_twist = angle_table(outer_size, inner_size, length)
    cos_inner, sin_inner = angle_table(inner_size, inner_size, inner_size)
    real_part = jnp.einsum("...ab,ak->...kb", shaped, cos_outer, precision=HIGHEST)
    imag_part = -jnp.einsum("...ab,ak->...kb", shaped, sin_outer, precision=HIGHEST)
    twist_real = real_part * cos_twist + imag_part * sin_twist
    twist_imag = imag_part * cos_twist - real_part * sin_twist
    out_real = jnp.einsum("...kb,bq->...kq", twist_real, cos_inner, precision=HIGHEST) + jnp.einsum(
        "...kb,bq->...kq", twist_imag, sin_inner, precision=HIGHEST
    )
    out_imag = jnp.einsum("...kb,bq->...kq", twist_imag, cos_inner, precision=HIGHEST) - jnp.einsum(
        "...kb,bq->...kq", twist_real, sin_inner, precision=HIGHEST
    )
    return (out_real, out_imag)


def inverse_dft(real_part, imag_part):
    outer_size = real_part.shape[-2]
    inner_size = real_part.shape[-1]
    length = outer_size * inner_size
    cos_outer, sin_outer = angle_table(outer_size, outer_size, outer_size)
    cos_twist, sin_twist = angle_table(outer_size, inner_size, length)
    cos_inner, sin_inner = angle_table(inner_size, inner_size, inner_size)
    step_real = jnp.einsum("...kq,qn->...kn", real_part, cos_inner, precision=HIGHEST) - jnp.einsum(
        "...kq,qn->...kn", imag_part, sin_inner, precision=HIGHEST
    )
    step_imag = jnp.einsum("...kq,qn->...kn", real_part, sin_inner, precision=HIGHEST) + jnp.einsum(
        "...kq,qn->...kn", imag_part, cos_inner, precision=HIGHEST
    )
    twist_real = step_real * cos_twist - step_imag * sin_twist
    twist_imag = step_real * sin_twist + step_imag * cos_twist
    result = jnp.einsum("...kn,ka->...an", twist_real, cos_outer, precision=HIGHEST) - jnp.einsum(
        "...kn,ka->...an", twist_imag, sin_outer, precision=HIGHEST
    )
    return result.reshape(result.shape[:-2] + (length,)) / length


def blocked_conv(signal, kernel, long_flag):
    chan_width, length = signal.shape
    block_count = length // SHORT
    blocks = signal.reshape(chan_width, block_count, SHORT)
    padded = jnp.concatenate([blocks, jnp.zeros_like(blocks)], axis=2)
    lagged = jnp.concatenate([jnp.zeros((chan_width, SHORT), jnp.float32), kernel], axis=1).reshape(
        chan_width, block_count + 1, SHORT
    )
    windows = jnp.concatenate([lagged[:, :-1], lagged[:, 1:]], axis=2)
    sig_real, sig_imag = forward_dft(padded)
    fil_real, fil_imag = forward_dft(windows)
    empty_freq = jnp.zeros_like(sig_real)
    pad_real = jnp.concatenate([empty_freq, sig_real], axis=1)
    pad_imag = jnp.concatenate([empty_freq, sig_imag], axis=1)

    def accumulate(shift_step, totals):
        keep_flag = jnp.where(shift_step == 0, 1.0, long_flag)
        moved_real = lax.dynamic_slice_in_dim(
            pad_real, block_count - shift_step, block_count, axis=1
        )
        moved_imag = lax.dynamic_slice_in_dim(
            pad_imag, block_count - shift_step, block_count, axis=1
        )
        part_real = lax.dynamic_slice_in_dim(fil_real, shift_step, 1, axis=1) * keep_flag
        part_imag = lax.dynamic_slice_in_dim(fil_imag, shift_step, 1, axis=1) * keep_flag
        return (
            totals[0] + moved_real * part_real - moved_imag * part_imag,
            totals[1] + moved_real * part_imag + moved_imag * part_real,
        )

    total_real, total_imag = lax.fori_loop(0, block_count, accumulate, (empty_freq, empty_freq))
    result = inverse_dft(total_real, total_imag)
    return result[:, :, SHORT:].reshape(chan_width, length)


def short_mix(projected, tap_weights, doc_pos):
    summed = tap_weights[0][:, :, None] * projected
    for lag_count in (1, 2):
        shifted = jnp.concatenate(
            [
                jnp.zeros(projected.shape[:2] + (lag_count,), jnp.float32),
                projected[:, :, :-lag_count],
            ],
            axis=2,
        )
        summed = (
            summed
            + tap_weights[lag_count][:, :, None]
            * shifted
            * (doc_pos >= lag_count).astype(jnp.float32)[None, None, :]
        )
    return summed


def mixer(
    projected, raw_filter, tap_weights, conv_shift, kind_here, stop_here, span_here, decay_rates
):
    length = projected.shape[2]
    offsets = jnp.arange(length, dtype=jnp.int32)
    doc_pos = jnp.where(kind_here == 1, offsets, offsets % SHORT)
    shorted = short_mix(projected, tap_weights, doc_pos)
    signal = shorted[0] * shorted[2]
    damping = jnp.exp(
        -offsets.astype(jnp.float32)[None, :] * decay_rates[:, None] / span_here.astype(jnp.float32)
    )
    inside = (offsets < stop_here).astype(jnp.float32)[None, :]
    kernel = raw_filter * damping * inside
    mixed_out = (
        blocked_conv(signal, kernel, kind_here.astype(jnp.float32)) + conv_shift[:, None] * signal
    )
    return shorted[1] * mixed_out


def local(
    tokens_in,
    ln_gain,
    ln_bias,
    in_weight,
    short_weight,
    filter_first,
    filter_mid,
    filter_last,
    conv_bias,
    out_weight,
    up_weight,
    down_weight,
    group_kind,
    filt_len,
    decay_win,
    cotangent,
):
    chan_count = lax.axis_size("chan")
    seq_count = lax.axis_size("seq")
    seq_index = lax.axis_index("seq")
    chan_index = lax.axis_index("chan")
    local_rows, width = tokens_in.shape
    group_len = local_rows * chan_count // 2
    spread = group_len // seq_count
    chan_width = conv_bias.shape[1]
    kinds = lax.dynamic_slice_in_dim(group_kind, 2 * seq_index, 2)
    stops = lax.dynamic_slice_in_dim(filt_len, 2 * seq_index, 2)
    spans = lax.dynamic_slice_in_dim(decay_win, 2 * seq_index, 2)
    global_chan = (chan_index * chan_width + jnp.arange(chan_width, dtype=jnp.int32)).astype(
        jnp.float32
    )
    decay_rates = jnp.exp(jnp.log(0.3) + jnp.log(100.0) * global_chan / (width - 1))
    positions = (seq_index * spread + jnp.arange(spread, dtype=jnp.int32)).astype(jnp.float32)
    features = position_features(positions, group_len)

    def mix_groups(proj_all, raw_all, taps, shift_all):

        def one_group(proj_one, kind_one, stop_one, span_one):
            return mixer(
                proj_one, raw_all, taps, shift_all, kind_one, stop_one, span_one, decay_rates
            )

        shaped = proj_all.reshape(3, chan_width, 2, group_len)
        mixed = jax.vmap(one_group, in_axes=(2, 0, 0, 0), out_axes=1)(shaped, kinds, stops, spans)
        return mixed.reshape(chan_width, 2 * group_len)

    stream = tokens_in
    kept_items = []
    for layer_index in range(LAYERS):
        gathered = (
            lax.all_gather(in_weight[layer_index], "chan", axis=0, tiled=True),
            lax.all_gather(out_weight[layer_index], "chan", axis=0, tiled=True),
            lax.all_gather(up_weight[layer_index], "chan", axis=0, tiled=True),
            lax.all_gather(down_weight[layer_index], "chan", axis=0, tiled=True),
            lax.all_gather(ln_gain[layer_index], "chan", axis=1, tiled=True),
            lax.all_gather(ln_bias[layer_index], "chan", axis=1, tiled=True),
        )
        w_in, w_out, w_up, w_down, gain_rows, shift_rows = gathered
        gain_rows = gain_rows.astype(jnp.float32)
        shift_rows = shift_rows.astype(jnp.float32)
        first_norm, first_back = jax.vjp(layer_norm, stream, gain_rows[0], shift_rows[0])
        normed_in = first_norm.astype(jnp.bfloat16)
        proj_cols = dot_cross(w_in, normed_in).astype(jnp.bfloat16).reshape(3, width, local_rows)
        by_channel = lax.all_to_all(proj_cols, "chan", split_axis=1, concat_axis=2, tiled=True)
        raw_local, filter_back = jax.vjp(
            lambda a, b, c: filter_columns(features, a, b, c),
            filter_first[layer_index],
            filter_mid[layer_index],
            filter_last[layer_index],
        )
        raw_whole = lax.all_gather(
            raw_local.astype(jnp.bfloat16), "seq", axis=1, tiled=True
        ).astype(jnp.float32)
        mixed_out, mixer_back = jax.vjp(
            mix_groups,
            by_channel.astype(jnp.float32),
            raw_whole,
            short_weight[layer_index],
            conv_bias[layer_index],
        )
        by_token = lax.all_to_all(
            mixed_out.astype(jnp.bfloat16), "chan", split_axis=1, concat_axis=0, tiled=True
        )
        middle_stream = stream + dot_lead(by_token, w_out)
        second_norm, second_back = jax.vjp(layer_norm, middle_stream, gain_rows[1], shift_rows[1])
        normed_mid = second_norm.astype(jnp.bfloat16)
        pre_act = jnp.dot(normed_mid, w_up, preferred_element_type=jnp.float32)
        hidden = jax.nn.gelu(pre_act, approximate=False).astype(jnp.bfloat16)
        stream = middle_stream + jnp.dot(hidden, w_down, preferred_element_type=jnp.float32)
        held_weights = None
        kept_items.append(
            (
                held_weights,
                first_back,
                normed_in,
                filter_back,
                mixer_back,
                by_token,
                second_back,
                normed_mid,
                pre_act,
                hidden,
            )
        )
    grad_stream = cotangent
    layer_grads = [None] * LAYERS
    local_grads = [None] * LAYERS
    for layer_index in reversed(range(LAYERS)):
        (
            held_weights,
            first_back,
            normed_in,
            filter_back,
            mixer_back,
            by_token,
            second_back,
            normed_mid,
            pre_act,
            hidden,
        ) = kept_items[layer_index]
        w_in, w_out, w_up, w_down = (
            lax.all_gather(in_weight[layer_index], "chan", axis=0, tiled=True),
            lax.all_gather(out_weight[layer_index], "chan", axis=0, tiled=True),
            lax.all_gather(up_weight[layer_index], "chan", axis=0, tiled=True),
            lax.all_gather(down_weight[layer_index], "chan", axis=0, tiled=True),
        )
        down_grad = grad_stream.astype(jnp.bfloat16)
        grad_w_down = dot_lead(hidden, down_grad)
        grad_hidden = dot_trail(down_grad, w_down)
        slope_grad = jax.vjp(lambda a: jax.nn.gelu(a, approximate=False), pre_act)[1](grad_hidden)[
            0
        ]
        up_grad = slope_grad.astype(jnp.bfloat16)
        grad_w_up = dot_lead(normed_mid, up_grad)
        grad_normed = dot_trail(up_grad, w_up)
        grad_mid, grad_gain_two, grad_shift_two = second_back(grad_normed)
        grad_mid = grad_stream + grad_mid
        out_grad = grad_mid.astype(jnp.bfloat16)
        grad_w_out = jnp.dot(by_token, out_grad, preferred_element_type=jnp.float32)
        grad_gated = dot_trail(w_out, out_grad).astype(jnp.bfloat16)
        grad_channel = lax.all_to_all(
            grad_gated, "chan", split_axis=0, concat_axis=1, tiled=True
        ).astype(jnp.float32)
        grad_proj, grad_raw, grad_taps, grad_cshift = mixer_back(grad_channel)
        proj_grad = lax.all_to_all(
            grad_proj.astype(jnp.bfloat16), "chan", split_axis=2, concat_axis=1, tiled=True
        ).reshape(3 * width, local_rows)
        grad_w_in = dot_cross(normed_in, proj_grad)
        grad_normed_in = dot_cross(proj_grad, w_in)
        grad_input, grad_gain_one, grad_shift_one = first_back(grad_normed_in)
        grad_stream = grad_mid + grad_input
        raw_grad = lax.psum_scatter(
            grad_raw.astype(jnp.bfloat16), "seq", scatter_dimension=1, tiled=True
        ).astype(jnp.float32)
        grad_first, grad_middle, grad_last = filter_back(raw_grad)
        gain_pair = jnp.stack([grad_gain_one, grad_gain_two])
        shift_pair = jnp.stack([grad_shift_one, grad_shift_two])
        layer_grads[layer_index] = (
            lax.psum_scatter(grad_w_in, "chan", scatter_dimension=0, tiled=True),
            lax.psum_scatter(grad_w_out, "chan", scatter_dimension=0, tiled=True),
            lax.psum_scatter(grad_w_up, "chan", scatter_dimension=0, tiled=True),
            lax.psum_scatter(grad_w_down, "chan", scatter_dimension=0, tiled=True),
            lax.psum_scatter(gain_pair, "chan", scatter_dimension=1, tiled=True),
            lax.psum_scatter(shift_pair, "chan", scatter_dimension=1, tiled=True),
        )
        local_grads[layer_index] = (grad_taps, grad_cshift, grad_last, grad_first, grad_middle)
    stack_in = jnp.stack([layer_grads[i][0] for i in range(LAYERS)])
    stack_out = jnp.stack([layer_grads[i][1] for i in range(LAYERS)])
    stack_up = jnp.stack([layer_grads[i][2] for i in range(LAYERS)])
    stack_down = jnp.stack([layer_grads[i][3] for i in range(LAYERS)])
    stack_gain = jnp.stack([layer_grads[i][4] for i in range(LAYERS)])
    stack_shift = jnp.stack([layer_grads[i][5] for i in range(LAYERS)])
    taps_all = jnp.stack([local_grads[i][0] for i in range(LAYERS)])
    cshift_all = jnp.stack([local_grads[i][1] for i in range(LAYERS)])
    last_all = jnp.stack([local_grads[i][2] for i in range(LAYERS)])
    first_all = jnp.stack([local_grads[i][3] for i in range(LAYERS)])
    middle_all = jnp.stack([local_grads[i][4] for i in range(LAYERS)])
    summed = (
        lax.psum(stack_in.astype(jnp.bfloat16), "seq").astype(jnp.float32),
        lax.psum(stack_out.astype(jnp.bfloat16), "seq").astype(jnp.float32),
        lax.psum(stack_up.astype(jnp.bfloat16), "seq").astype(jnp.float32),
        lax.psum(stack_down.astype(jnp.bfloat16), "seq").astype(jnp.float32),
        lax.psum(stack_gain.astype(jnp.bfloat16), "seq").astype(jnp.float32),
        lax.psum(stack_shift.astype(jnp.bfloat16), "seq").astype(jnp.float32),
        lax.psum(taps_all.astype(jnp.bfloat16), "seq").astype(jnp.float32),
        lax.psum(cshift_all.astype(jnp.bfloat16), "seq").astype(jnp.float32),
        lax.psum(last_all.astype(jnp.bfloat16), "seq").astype(jnp.float32),
    )
    core_sums = lax.psum((first_all, middle_all), ("seq", "chan"))
    return (
        stream,
        grad_stream,
        summed[4],
        summed[5],
        summed[0],
        summed[6],
        core_sums[0],
        core_sums[1],
        summed[8],
        summed[7],
        summed[1],
        summed[2],
        summed[3],
    )


def solution(mesh):
    in_specs = (
        P(("seq", "chan"), None),
        P(None, None, "chan"),
        P(None, None, "chan"),
        P(None, "chan", None),
        P(None, None, None, "chan"),
        P(),
        P(),
        P(None, None, "chan"),
        P(None, "chan"),
        P(None, "chan", None),
        P(None, "chan", None),
        P(None, "chan", None),
        P(),
        P(),
        P(),
        P(("seq", "chan"), None),
    )
    out_specs = (
        P(("seq", "chan"), None),
        P(("seq", "chan"), None),
        P(None, None, "chan"),
        P(None, None, "chan"),
        P(None, "chan", None),
        P(None, None, None, "chan"),
        P(),
        P(),
        P(None, None, "chan"),
        P(None, "chan"),
        P(None, "chan", None),
        P(None, "chan", None),
        P(None, "chan", None),
    )
    return jax.shard_map(local, mesh=mesh, in_specs=in_specs, out_specs=out_specs, check_vma=False)
```

profile of v0, /device:TPU:0, one launch (start us, length us, event | category | flops | bytes accessed | tf_op | source)
XLA Modules:
  0.0 4954.0 jit_solution(9939556210126302134)
XLA Ops:
  215.4 182.0 %all-to-all-done = bf16[3,1024,1024]{2,0,1:T(4,128)(2,1)} async-done(((bf16[3,1024,1024]{2,0,1:T(4,128)(2,1)}), bf16[3,1024,1024]{2,0,1:T(4,128)(2,1)}, u32[]{:S(2)}, u32[]{:S(2)}) %all-to-all-start) | async-done | bytes 6291488 | tf_op jit(solution)/shard_map/all_to_all | solution.py:252
  504.0 32.3 add_bitcast_fusion.8
  694.7 197.4 %while.134 = (s32[]{:T(128)}, f32[2,128,2,32,128]{4,3,2,1,0:T(8,128)}, f32[2,128,2,32,128]{4,3,2,1,0:T(8,128)}, s32[2,4]{1,0:T(2,128)S(1)}, s32[2,4]{1,0:T(2,128...) while((s32[]{:T(128)}, ...), condition=%wide.region_3.4_spmd.clone, body=%wide.region_2.3_spmd.clone.sunk | while | flops 25165848 | bytes 243272656 | solution.py:145
  763.8 23.2 fusion.925
  847.4 25.6 fusion.925
  938.3 24.0 multiply_subtract_fusion.1
  1027.1 65.0 %all-gather.6 = bf16[1,2,1024]{2,1,0:T(2,128)(2,1)S(1)} all-gather(bf16[1,2,128]{2,1,0:T(2,128)(2,1)S(1)} %copy-done.202), channel_id=8, replica_groups=mesh['seq'=4,'chan'=8] {'chan'}, dimensions={2}, use_global_device_ids=true | all-gather | bytes 4608 | tf_op jit(solution)/shard_map/all_gather | solution.py:243
  1092.1 41.3 all-gather.7
  1146.0 47.3 multiply_convert_fusion.1
  1310.4 206.7 %all-to-all-done.2 = bf16[3,1024,1024]{2,0,1:T(4,128)(2,1)} async-done(((bf16[3,1024,1024]{2,0,1:T(4,128)(2,1)}), bf16[3,1024,1024]{2,0,1:T(4,128)(2,1)}, u32[]{:S(2)}, u32[]{:S(2)}) %all-to-all-start.2) | async-done | bytes 6291488 | tf_op jit(solution)/shard_map/all_to_all | solution.py:252
  1739.2 196.8 %while.135 = (s32[]{:T(128)}, f32[2,128,2,32,128]{4,3,2,1,0:T(8,128)}, f32[2,128,2,32,128]{4,3,2,1,0:T(8,128)}, s32[2,4]{1,0:T(2,128)S(1)}, s32[2,4]{1,0:T(2,128...) while((s32[]{:T(128)}, ...), condition=%wide.region_9.10_spmd.clone, body=%wide.region_8.9_spmd.clone.sunk | while | flops 25165848 | bytes 243272656 | solution.py:145
  1807.9 23.3 fusion.928
  1891.2 25.6 fusion.928
  1982.1 24.1 multiply_subtract_fusion
  2074.5 88.0 %all-to-all-done.3 = bf16[128,8,1024]{0,2,1:T(8,128)(2,1)S(1)} async-done(((bf16[128,8,1024]{0,2,1:T(8,128)(2,1)}), bf16[128,8,1024]{0,2,1:T(8,128)(2,1)S(1)}, u32[]{:S(2)}, u32[]{:S(2)}) %all-to-all-start.3) | async-done | bytes 2097184 | tf_op jit(solution)/shard_map/all_to_all | solution.py:269
  2173.7 47.4 multiply_convert_fusion
  2221.1 23.8 add_convert_fusion.1
  2287.6 49.0 all-to-all-done.4
  2392.7 24.2 fusion.268
  2416.9 23.6 fusion.123
  2440.5 28.7 fusion.824
  2492.6 23.6 convolution_add_fusion.3
  2552.1 213.1 %while.132 = (s32[]{:T(128)}, f32[2,128,4,32,128]{4,1,3,2,0:T(8,128)}, f32[2,128,4,32,128]{4,1,3,2,0:T(8,128)}, f32[2,128,2,32,128]{4,1,3,2,0:T(8,128)}, f32[2,1...) while((s32[]{:T(128)}, ...), condition=%wide.region_21.22_spmd, body=%wide.region_14.21_spmd.sunk | while | flops 41943100 | bytes 369101440 | solution.py:145
  2576.8 37.9 fusion.915
  2683.0 37.9 fusion.915
  2848.1 34.4 negate_bitcast_fusion
  2945.9 25.4 multiply_reduce_fusion.2
  3003.7 39.9 copy.451
  3054.8 217.1 %all-to-all-done.5 = bf16[3,128,8192]{1,0,2:T(4,128)(2,1)} async-done(((bf16[3,128,8192]{1,0,2:T(4,128)(2,1)}), bf16[3,128,8192]{1,0,2:T(4,128)(2,1)}, u32[]{:S(2)}, u32[]{:S(2)}) %all-to-all-start.5) | async-done | bytes 6291488 | tf_op jit(solution)/shard_map/all_to_all | solution.py:333
  3318.3 23.5 add_convert_fusion
  3472.6 67.0 %all-to-all-done.6 = bf16[8,128,1024]{1,2,0:T(8,128)(2,1)S(1)} async-done(((bf16[8,128,1024]{1,2,0:T(8,128)(2,1)}), bf16[8,128,1024]{1,2,0:T(8,128)(2,1)S(1)}, u32[]{:S(2)}, u32[]{:S(2)}) %all-to-all-start.6) | async-done | bytes 2097184 | tf_op jit(solution)/shard_map/all_to_all | solution.py:329
  3597.2 23.9 fusion.271
  3621.2 23.6 fusion.117
  3644.8 28.8 fusion.825
  3697.1 23.8 convolution_add_fusion.1
  3757.3 218.8 %while.133 = (s32[]{:T(128)}, f32[2,128,4,32,128]{4,1,3,2,0:T(8,128)}, f32[2,128,4,32,128]{4,1,3,2,0:T(8,128)}, f32[2,128,2,32,128]{4,1,3,2,0:T(8,128)}, f32[2,1...) while((s32[]{:T(128)}, ...), condition=%wide.region_33.34_spmd, body=%wide.region_26.33_spmd.sunk | while | flops 41943100 | bytes 369101440 | solution.py:145
  3782.2 38.3 fusion.920
  3890.7 38.6 fusion.920
  4059.4 35.2 negate_bitcast_fusion.1
  4158.6 25.8 multiply_reduce_fusion.5
  4217.9 39.9 copy.468
  4257.8 195.0 %all_to_all.106 = bf16[3,128,8192]{1,0,2:T(4,128)(2,1)S(1)} all-to-all(bf16[3,128,8192]{1,0,2:T(4,128)(2,1)S(1)} %copy.468), channel_id=1, replica_groups=mesh['seq'=4,'chan'=8] {'chan'}, dimensions={2} | all-to-all | bytes 12582912 | tf_op jit(solution)/shard_map/all_to_all | solution.py:333
  4493.8 18.0 add_bitcast_fusion
  4547.2 17.7 add_bitcast_fusion.2
  4669.6 27.8 reduce-scatter.29.cloned.1.call-done
  4701.0 27.9 reduce-scatter.27.cloned.1.call-done
  4733.2 41.1 all-reduce.34
  4814.7 121.1 %all-reduce.39.cloned.1.call-done = (bf16[2,128,3072]{2,1,0:T(8,128)(2,1)}, bf16[2,128,1024]{2,1,0:T(8,128)(2,1)}, bf16[2,128,4096]{2,1,0:T(8,128)(2,1)}, bf16[2,512,1024]{2,1,0:T(8,128)(2,1)}) async-done(((bf16[2,128,3072]{2,1,0:T(8,128)(2,1)}, bf16[2,128,1024]{2,1,0:T(8,128)(2,1)}, bf16[2,128,4096]{2,1,0:T(8,128)(2,1)}, bf16[2,512,1024]{2,1,0:T(8,128)(2,1)}), (bf16[2,128,3072]{2,1,0:T(8,128)(2,1)}, ...) | async-done | bytes 6291472 | tf_op jit(solution)/shard_map/psum | solution.py:367
  (1111 shorter events, 2641.3 us)
Async XLA Ops:
  7.2 70.6 %all-gather.27.cloned.1.call-start = ((), (), s32[]{:S(2)}) async-start(), calls=%async_computation.34 | async-start | bytes 7077888 | tf_op jit(solution)/shard_map/all_gather | solution.py:239
  10.0 109.7 %all-gather.23.cloned.1.call-start = ((), (), s32[]{:S(2)}) async-start(), calls=%async_computation.22 | async-start | bytes 1310720 | tf_op jit(solution)/shard_map/all_gather | solution.py:259
  19.8 114.7 %all-gather.25.cloned.1.call-start = ((), (), s32[]{:S(2)}) async-start(), calls=%async_computation.23 | async-start | bytes 1310720 | tf_op jit(solution)/shard_map/all_gather | solution.py:259
  28.4 1109.1 %all-gather.29.cloned.1.call-start = ((), (), s32[]{:S(2)}) async-start(), calls=%async_computation.35 | async-start | bytes 2359296 | tf_op jit(solution)/shard_map/all_gather | solution.py:240
  29.3 1116.7 %all-gather.31.cloned.1.call-start = ((), (), s32[]{:S(2)}) async-start(), calls=%async_computation.36 | async-start | bytes 9437184 | tf_op jit(solution)/shard_map/all_gather | solution.py:241
  30.8 1162.5 %all-gather.33.cloned.1.call-start = ((), (), s32[]{:S(2)}) async-start(), calls=%async_computation.37 | async-start | bytes 9437184 | tf_op jit(solution)/shard_map/all_gather | solution.py:242
  110.6 286.8 %all-to-all-start = ((bf16[3,1024,1024]{2,0,1:T(4,128)(2,1)}), bf16[3,1024,1024]{2,0,1:T(4,128)(2,1)}, u32[]{:S(2)}, u32[]{:S(2)}) async-start(bf16[3,1024,1024]{2,0,1:T(4,128)(2,1)} %copy.370), calls=%async_computation | async-start | bytes 16777216 | tf_op jit(solution)/shard_map/all_to_all | solution.py:252
  117.1 386.9 %copy-start.47 = (f32[32,128]{1,0:T(8,128)}, f32[32,128]{1,0:T(8,128)S(1)}, u32[]{:S(2)}) copy-start(f32[32,128]{1,0:T(8,128)S(1)} %get-tuple-element.2558) | copy-start | bytes 49156
  117.1 386.9 %copy-start.55 = (f32[32,128]{1,0:T(8,128)}, f32[32,128]{1,0:T(8,128)S(1)}, u32[]{:S(2)}) copy-start(f32[32,128]{1,0:T(8,128)S(1)} %get-tuple-element.2559) | copy-start | bytes 49156
  118.8 323.5 %copy-start.153 = (f32[3,128]{1,0:T(4,128)}, f32[3,128]{1,0:T(4,128)S(1)}, u32[]{:S(2)}) copy-start(f32[3,128]{1,0:T(4,128)S(1)} %get-tuple-element.2555) | copy-start | bytes 4612
  118.8 323.5 %copy-start.151 = (f32[3,128]{1,0:T(4,128)}, f32[3,128]{1,0:T(4,128)S(1)}, u32[]{:S(2)}) copy-start(f32[3,128]{1,0:T(4,128)S(1)} %get-tuple-element.2557) | copy-start | bytes 4612
  118.8 323.5 %copy-start.155 = (f32[3,128]{1,0:T(4,128)}, f32[3,128]{1,0:T(4,128)S(1)}, u32[]{:S(2)}) copy-start(f32[3,128]{1,0:T(4,128)S(1)} %get-tuple-element.2556) | copy-start | bytes 4612
  119.0 323.3 %copy-start.86 = (f32[2,4096]{1,0:T(2,128)}, f32[2,4096]{1,0:T(2,128)S(1)}, u32[]{:S(2)}) copy-start(f32[2,4096]{1,0:T(2,128)S(1)} %get-tuple-element.2500) | copy-start | bytes 98308
  119.0 323.3 %copy-start.90 = (f32[2,4096]{1,0:T(2,128)}, f32[2,4096]{1,0:T(2,128)S(1)}, u32[]{:S(2)}) copy-start(f32[2,4096]{1,0:T(2,128)S(1)} %get-tuple-element.2501) | copy-start | bytes 98308
  1012.8 79.3 %copy-start.203 = (bf16[1,2,128]{2,1,0:T(2,128)(2,1)S(1)}, bf16[1,2,128]{2,1,0:T(2,128)(2,1)}, u32[]{:S(2)}) copy-start(bf16[1,2,128]{2,1,0:T(2,128)(2,1)} %get-tuple-element.2522) | copy-start | bytes 1540
  1020.7 114.0 %all-to-all-start.1 = ((bf16[128,8,1024]{0,2,1:T(8,128)(2,1)}), bf16[128,8,1024]{0,2,1:T(8,128)(2,1)S(1)}, u32[]{:S(2)}, u32[]{:S(2)}) async-start(bf16[128,8,1024]{0,2,1:T(8,128)(2,1)} %bitcast.1051), calls=%async_computation.1 | async-start | bytes 4194304 | tf_op jit(solution)/shard_map/all_to_all | solution.py:269
  1026.3 184.3 %all-gather.35.cloned.1.call-start = ((), (), s32[]{:S(2)}) async-start(), calls=%async_computation.38 | async-start | bytes 7077888 | tf_op jit(solution)/shard_map/all_gather | solution.py:239
  1243.7 273.3 %all-to-all-start.2 = ((bf16[3,1024,1024]{2,0,1:T(4,128)(2,1)}), bf16[3,1024,1024]{2,0,1:T(4,128)(2,1)}, u32[]{:S(2)}, u32[]{:S(2)}) async-start(bf16[3,1024,1024]{2,0,1:T(4,128)(2,1)} %copy.404), calls=%async_computation.2 | async-start | bytes 16777216 | tf_op jit(solution)/shard_map/all_to_all | solution.py:252
  1248.9 916.2 %all-gather.37.cloned.1.call-start = ((), (), s32[]{:S(2)}) async-start(), calls=%async_computation.39 | async-start | bytes 2359296 | tf_op jit(solution)/shard_map/all_gather | solution.py:240
  1249.6 924.1 %all-gather.39.cloned.1.call-start = ((), (), s32[]{:S(2)}) async-start(), calls=%async_computation.40 | async-start | bytes 9437184 | tf_op jit(solution)/shard_map/all_gather | solution.py:241
  1250.4 311.5 %copy-start.159 = (f32[3,128]{1,0:T(4,128)}, f32[3,128]{1,0:T(4,128)S(1)}, u32[]{:S(2)}) copy-start(f32[3,128]{1,0:T(4,128)S(1)} %get-tuple-element.2553) | copy-start | bytes 4612
  1250.4 311.5 %copy-start.161 = (f32[3,128]{1,0:T(4,128)}, f32[3,128]{1,0:T(4,128)S(1)}, u32[]{:S(2)}) copy-start(f32[3,128]{1,0:T(4,128)S(1)} %get-tuple-element.2552) | copy-start | bytes 4612
  2064.7 97.7 %all-to-all-start.3 = ((bf16[128,8,1024]{0,2,1:T(8,128)(2,1)}), bf16[128,8,1024]{0,2,1:T(8,128)(2,1)S(1)}, u32[]{:S(2)}, u32[]{:S(2)}) async-start(bf16[128,8,1024]{0,2,1:T(8,128)(2,1)} %bitcast.1052), calls=%async_computation.3 | async-start | bytes 4194304 | tf_op jit(solution)/shard_map/all_to_all | solution.py:269
  2068.3 152.8 %all-gather.41.cloned.1.call-start = ((), (), s32[]{:S(2)}) async-start(), calls=%async_computation.41 | async-start | bytes 9437184 | tf_op jit(solution)/shard_map/all_gather | solution.py:242
  2281.6 55.0 %all-to-all-start.4 = ((bf16[8,128,1024]{1,2,0:T(8,128)(2,1)}), bf16[8,128,1024]{1,2,0:T(8,128)(2,1)S(1)}, u32[]{:S(2)}, u32[]{:S(2)}) async-start(bf16[8,128,1024]{1,2,0:T(8,128)(2,1)} %copy.439), calls=%async_computation.4 | async-start | bytes 4194304 | tf_op jit(solution)/shard_map/all_to_all | solution.py:329
  3043.6 228.3 %all-to-all-start.5 = ((bf16[3,128,8192]{1,0,2:T(4,128)(2,1)}), bf16[3,128,8192]{1,0,2:T(4,128)(2,1)}, u32[]{:S(2)}, u32[]{:S(2)}) async-start(bf16[3,128,8192]{1,0,2:T(4,128)(2,1)} %copy.451), calls=%async_computation.5 | async-start | bytes 16777216 | tf_op jit(solution)/shard_map/all_to_all | solution.py:333
  3048.7 1540.9 %reduce-scatter.33.cloned.1.call-start = ((), (), s32[]{:S(2)}) async-start(), calls=%async_computation.29 | async-start | bytes 4718592 | tf_op jit(solution)/shard_map/reduce_scatter | solution.py:348
  3054.7 1536.0 %reduce-scatter.31.cloned.1.call-start = ((), (), s32[]{:S(2)}) async-start(), calls=%async_computation.28 | async-start | bytes 4718592 | tf_op jit(solution)/shard_map/reduce_scatter | solution.py:348
  3378.1 1242.6 %reduce-scatter.41.cloned.1.call-start = ((), (), s32[]{:S(2)}) async-start(), calls=%async_computation.33 | async-start | bytes 18874368 | tf_op jit(solution)/shard_map/reduce_scatter | solution.py:350
  3395.0 1227.4 %reduce-scatter.37.cloned.1.call-start = ((), (), s32[]{:S(2)}) async-start(), calls=%async_computation.31 | async-start | bytes 18874368 | tf_op jit(solution)/shard_map/reduce_scatter | solution.py:349
  3412.7 1211.4 %reduce-scatter.25.cloned.1.call-start = ((), (), s32[]{:S(2)}) async-start(), calls=%async_computation.25 | async-start | bytes 14155776 | tf_op jit(solution)/shard_map/reduce_scatter | solution.py:347
  3426.3 1199.4 %reduce-scatter.39.cloned.1.call-start = ((), (), s32[]{:S(2)}) async-start(), calls=%async_computation.32 | async-start | bytes 18874368 | tf_op jit(solution)/shard_map/reduce_scatter | solution.py:350
  3452.1 87.5 %all-to-all-start.6 = ((bf16[8,128,1024]{1,2,0:T(8,128)(2,1)}), bf16[8,128,1024]{1,2,0:T(8,128)(2,1)S(1)}, u32[]{:S(2)}, u32[]{:S(2)}) async-start(bf16[8,128,1024]{1,2,0:T(8,128)(2,1)} %copy.456), calls=%async_computation.6 | async-start | bytes 4194304 | tf_op jit(solution)/shard_map/all_to_all | solution.py:329
  3455.7 1173.4 %reduce-scatter.35.cloned.1.call-start = ((), (), s32[]{:S(2)}) async-start(), calls=%async_computation.30 | async-start | bytes 18874368 | tf_op jit(solution)/shard_map/reduce_scatter | solution.py:349
  3472.5 1159.8 %reduce-scatter.23.cloned.1.call-start = ((), (), s32[]{:S(2)}) async-start(), calls=%async_computation.24 | async-start | bytes 14155776 | tf_op jit(solution)/shard_map/reduce_scatter | solution.py:347
  4478.1 179.0 %reduce-scatter.49.cloned.1.call-start = ((), (), s32[]{:S(2)}) async-start(), calls=%async_computation.45 | async-start | bytes 589824
  4530.4 138.2 %reduce-scatter.45.cloned.1.call-start = ((), (), s32[]{:S(2)}) async-start(), calls=%async_computation.43 | async-start | bytes 589824
  4531.6 165.9 %reduce-scatter.29.cloned.1.call-start = ((), (), s32[]{:S(2)}) async-start(), calls=%async_computation.27 | async-start | bytes 1310720 | tf_op jit(solution)/shard_map/reduce_scatter | solution.py:340
  4589.5 139.4 %reduce-scatter.27.cloned.1.call-start = ((), (), s32[]{:S(2)}) async-start(), calls=%async_computation.26 | async-start | bytes 1310720 | tf_op jit(solution)/shard_map/reduce_scatter | solution.py:340
  4590.7 200.8 %reduce-scatter.47.cloned.1.call-start = ((), (), s32[]{:S(2)}) async-start(), calls=%async_computation.44 | async-start | bytes 589824
  4619.4 174.0 %reduce-scatter.43.cloned.1.call-start = ((), (), s32[]{:S(2)}) async-start(), calls=%async_computation.42 | async-start | bytes 589824
  4620.6 315.2 %all-reduce.39.cloned.1.call-start = ((), (), s32[]{:S(2)}) async-start(), calls=%async_computation.46 | async-start | bytes 12582912 | tf_op jit(solution)/shard_map/psum | solution.py:367
  4651.5 79.5 %copy-start.84 = (f32[1024,64]{0,1:T(8,128)S(1)}, f32[1024,64]{0,1:T(8,128)}, u32[]{:S(2)}) copy-start(f32[1024,64]{0,1:T(8,128)} %get-tuple-element.2529) | copy-start | bytes 786436
  4651.5 81.0 %copy-start.72 = (f32[1024,64]{0,1:T(8,128)S(1)}, f32[1024,64]{0,1:T(8,128)}, u32[]{:S(2)}) copy-start(f32[1024,64]{0,1:T(8,128)} %copy-done.71) | copy-start | bytes 786436
  4651.5 81.3 %copy-start.70 = (f32[1024,64]{0,1:T(8,128)S(1)}, f32[1024,64]{0,1:T(8,128)}, u32[]{:S(2)}) copy-start(f32[1024,64]{0,1:T(8,128)} %copy-done.69) | copy-start | bytes 786436
  4651.5 123.4 %copy-start.66 = (f32[1024,64]{0,1:T(8,128)S(1)}, f32[1024,64]{0,1:T(8,128)}, u32[]{:S(2)}) copy-start(f32[1024,64]{0,1:T(8,128)} %copy-done.65) | copy-start | bytes 786436
  4651.5 124.6 %copy-start.68 = (f32[1024,64]{0,1:T(8,128)S(1)}, f32[1024,64]{0,1:T(8,128)}, u32[]{:S(2)}) copy-start(f32[1024,64]{0,1:T(8,128)} %copy-done.67) | copy-start | bytes 786436
  4651.5 125.9 %copy-start.148 = (f32[1024]{0:T(1024)S(1)}, f32[1024]{0:T(1024)}, u32[]{:S(2)}) copy-start(f32[1024]{0:T(1024)} %copy-done.147) | copy-start | bytes 12292
  (265 other events, 3943.6 us)
Sparse Core Ops, SparseCore 0:
  10.2 67.5 all-gather.26
  80.2 25.2 all-gather.22
  107.9 26.6 all-gather.24
  136.0 54.9 all-gather.28
  192.5 175.6 all-gather.30
  369.6 84.1 all-gather.32
  1028.8 98.7 all-gather.34
  1251.3 45.8 all-gather.36
  1299.4 189.7 all-gather.38
  2070.4 115.8 all-gather.40
  3054.8 123.9 reduce-scatter.32
  3378.2 47.0 reduce-scatter.30
  3427.6 198.9 reduce-scatter.40
  3628.8 178.0 reduce-scatter.36
  3809.0 127.5 reduce-scatter.24
  3938.8 166.6 reduce-scatter.38
  4107.7 173.8 reduce-scatter.34
  4478.2 127.4 reduce-scatter.22
  4608.0 29.2 reduce-scatter.48
  4639.5 29.1 reduce-scatter.44
  4671.5 25.8 reduce-scatter.28
  4701.1 27.7 reduce-scatter.26
  4731.2 31.0 reduce-scatter.46
  4764.5 28.9 reduce-scatter.42
  4797.8 137.9 all-reduce.38
where the time goes:
time: 4970 us; the launch traced here: 4950 us
  matrix products  1530 us (31%)
  local copies, waits for them, and re-layouts  1150 us (23%)
  waiting for transfers between devices  1020 us (21%)
  other arithmetic  753 us (15%)
  blocking collectives  382 us (8%)
  loops' own time  57.2 us (1%)
    all_to_all x2, waiting for transfers between devices, local(): lax.all_to_all(proj_cols, 'chan', split_axis=1, concat_axis=2, tiled=True)  389 us
    all_to_all x1, waiting for transfers between devices, local(): lax.all_to_all(grad_proj.astype(jnp.bfloat16), 'chan', split_axis=2, conc...  217 us
    all_to_all x1, blocking collectives, local(): lax.all_to_all(grad_proj.astype(jnp.bfloat16), 'chan', split_axis=2, conc...  195 us
    another operation x46, local copies, waits for them, and re-layouts  185 us
    dot_general x8, matrix products, forward_dft(): jnp.einsum('...kb,bq->...kq', twist_imag, cos_inner, precision=HIGHEST)  160 us
    reduce_sum x4, other arithmetic, accumulate(): moved_imag * part_imag  153 us
    dot_general x8, matrix products, forward_dft(): jnp.einsum('...ab,ak->...kb', shaped, cos_outer, precision=HIGHEST)  129 us
    psum x1, waiting for transfers between devices, local(): lax.psum(stack_in.astype(jnp.bfloat16), 'seq').astype(jnp.float32)  121 us
  transfers between devices with their start and end apart: 32, of which 13 were waited for; matrix products, arithmetic and copies ran while one was open for 52% of the time, Pallas kernels for 0%

commit v1 on v0

--- a/solution.py
+++ b/solution.py
@@ -1,12 +1,27 @@
+import functools
 import math
 
 import jax
 import jax.numpy as jnp
+import ml_dtypes
+import numpy as np
 from jax import lax
+from jax.experimental import pallas as pl
+from jax.experimental.pallas import tpu as pltpu
+from jax.sharding import Mesh
 from jax.sharding import PartitionSpec as P
 
 LAYERS = 2
 SHORT = 2048
+BLOCK = 512
+HALF = BLOCK // 2
+TILE = 256
+EDGE = 16
+STRIP = 128
+MIB = 1 << 20
+F32 = jnp.float32
+BF16 = jnp.bfloat16
+LIGHT = pl.CostEstimate(flops=1000, bytes_accessed=1000, transcendentals=0)
 
 
 HIGHEST = lax.Precision.HIGHEST
@@ -392,38 +407,1576 @@
     )
 
 
+def transform_tables():
+    freq = np.concatenate([np.arange(0, HALF, 2), np.arange(1, HALF, 2)])
+    tables = []
+    for parity in range(2):
+        time = 2 * np.arange(HALF) + parity
+        turns = ((2 * freq[:, None] + 1) * time[None, :]) % (4 * BLOCK)
+        angles = turns * (np.pi / (2 * BLOCK))
+        tables.append(np.concatenate([np.cos(angles), -np.sin(angles)]))
+    table = np.stack(tables).astype(ml_dtypes.bfloat16)
+    return table, np.ascontiguousarray(table.transpose(0, 2, 1))
+
+
+def matmul(left, right):
+    return jnp.dot(left, right, preferred_element_type=F32)
+
+
+def row_slices():
+    return [pl.ds(k * HALF, HALF) for k in range(4)]
+
+
+def to_spectrum(dft_ref, even, odd, store):
+    even, odd = matmul(dft_ref[0], even), matmul(dft_ref[1], odd)
+    store(0, even[:HALF] + odd[:HALF])
+    store(1, even[:HALF] - odd[:HALF])
+    store(2, even[HALF:] + odd[HALF:])
+    store(3, odd[HALF:] - even[HALF:])
+
+
+def from_spectrum(inverse_ref, parts):
+    scale = 1.0 / BLOCK
+    even = jnp.concatenate([(parts[0] + parts[1]).astype(BF16), (parts[2] - parts[3]).astype(BF16)], axis=0)
+    odd = jnp.concatenate([(parts[0] - parts[1]).astype(BF16), (parts[2] + parts[3]).astype(BF16)], axis=0)
+    return matmul(inverse_ref[0], even) * scale, matmul(inverse_ref[1], odd) * scale
+
+
+def block_offsets(block):
+    row = lax.broadcasted_iota(jnp.int32, (BLOCK, TILE), 0)
+    return block * BLOCK + jnp.where(row < HALF, 2 * row, 2 * (row - HALF) + 1)
+
+
+def window_kernel(place_ref, hidden_ref, last_ref, rate_ref, dft_ref, out_ref, before, table):
+    d = pl.program_id(1)
+    slowness = rate_ref[...] / place_ref[4].astype(F32)
+
+    @pl.when(d == 0)
+    def _():
+        before[...] = jnp.zeros_like(before)
+        table[...] = jnp.exp(-block_offsets(0).astype(F32) * slowness)
+
+    @pl.when(d <= 2 * jnp.maximum(place_ref[0], place_ref[1]) + 1)
+    def _():
+        raw = matmul(hidden_ref[...], last_ref[...]).astype(BF16).astype(F32)
+        fade = jnp.exp(-(d * BLOCK).astype(F32) * slowness)
+        taps = jnp.where(block_offsets(d) < place_ref[3], raw * (table[...] * fade), 0.0).astype(BF16)
+        slices = row_slices()
+        now = [None] * 4
+
+        def keep(k, rows):
+            now[k] = rows
+
+        to_spectrum(dft_ref, taps[:HALF], taps[HALF:], keep)
+        sign = jnp.where(lax.broadcasted_iota(jnp.int32, (HALF, TILE), 0) < HALF // 2, 1.0, -1.0)
+        out_ref[0, slices[0], :] = (now[0] - sign * before[slices[2], :]).astype(BF16)
+        out_ref[0, slices[1], :] = (now[1] + sign * before[slices[3], :]).astype(BF16)
+        out_ref[0, slices[2], :] = (now[2] + sign * before[slices[0], :]).astype(BF16)
+        out_ref[0, slices[3], :] = (now[3] - sign * before[slices[1], :]).astype(BF16)
+        for k in range(4):
+            before[slices[k], :] = now[k]
+
+
+def window_spectra(place, hidden, last, rates, dft):
+    length, inner = hidden.shape
+    width = last.shape[1]
+    count = length // BLOCK
+    return pl.pallas_call(
+        window_kernel,
+        grid_spec=pltpu.PrefetchScalarGridSpec(
+            num_scalar_prefetch=1,
+            grid=(width // TILE, count),
+            in_specs=[
+                pl.BlockSpec((BLOCK, inner), lambda c, d, *_: (d, 0)),
+                pl.BlockSpec((inner, TILE), lambda c, d, *_: (0, c)),
+                pl.BlockSpec((1, TILE), lambda c, d, *_: (0, c)),
+                pl.BlockSpec(dft.shape, lambda c, d, *_: (0, 0, 0)),
+            ],
+            out_specs=pl.BlockSpec((1, 2 * BLOCK, TILE), lambda c, d, *_: (d, 0, c)),
+            scratch_shapes=[pltpu.VMEM((2 * BLOCK, TILE), F32), pltpu.VMEM((BLOCK, TILE), F32)],
+        ),
+        out_shape=jax.ShapeDtypeStruct((count, 2 * BLOCK, width), BF16),
+        compiler_params=pltpu.CompilerParams(vmem_limit_bytes=32 * MIB),
+        cost_estimate=LIGHT,
+        name="window_spectra",
+    )(place, hidden, last, rates, dft)
+
+
+ROWS_STEP = 16
+
+
+def load_pair(ref, block, base):
+    real = ref[block, pl.ds(base, ROWS_STEP), :].astype(F32)
+    imag = ref[block, pl.ds(BLOCK + base, ROWS_STEP), :].astype(F32)
+    return real, imag
+
+
+def add_pair(ref, block, base, real, imag):
+    ref[block, pl.ds(base, ROWS_STEP), :] += real
+    ref[block, pl.ds(BLOCK + base, ROWS_STEP), :] += imag
+
+
+def product(a, b):
+    return a[0] * b[0] - a[1] * b[1], a[0] * b[1] + a[1] * b[0]
+
+
+def conj_product(a, b):
+    return a[0] * b[0] + a[1] * b[1], a[0] * b[1] - a[1] * b[0]
+
+
+def plus(a, b):
+    return a[0] + b[0], a[1] + b[1]
+
+
+def interleave(woven, block, parity, rows):
+    for side in range(TILE // 128):
+        at = pl.ds(block * BLOCK + parity, HALF, stride=2)
+        woven[side, at, :] = rows[:, side * 128 : side * 128 + 128]
+
+
+def transform_blocks(dft_ref, target, source):
+    for b in range(2):
+        slices = row_slices()
+
+        def store(k, rows, b=b, slices=slices):
+            target[b, slices[k], :] = rows
+
+        to_spectrum(
+            dft_ref, source[pl.ds(b * BLOCK, HALF), :], source[pl.ds(b * BLOCK + HALF, HALF), :], store
+        )
+
+
+def over_rows(body):
+    def one(index, carry):
+        body(pl.multiple_of(index * ROWS_STEP, ROWS_STEP))
+        return carry
+
+    lax.fori_loop(0, BLOCK // ROWS_STEP, one, 0, unroll=8)
+
+
+def each_hop(place_ref, later, body):
+    hops = place_ref[1] if later else place_ref[0]
+    near = place_ref[2] == (0 if later else 1)
+    pl.when((hops >= 1) & near)(lambda: body(1, 1))
+    pl.when((hops >= 1) & jnp.logical_not(near))(lambda: body(1, 3))
+    pl.when(hops >= 2)(lambda: body(2, 2))
+    pl.when(hops >= 3)(lambda: body(3, 3))
+
+
+def conv_forward_kernel(
+    place_ref, own, partner, far, beyond, window_ref, dft_ref, inverse_ref, gate_ref, shift_ref,
+    gated_ref, conv_ref, spec, total, woven,
+):
+    sources = (own, partner, far, beyond)
+
+    def transform(source):
+        transform_blocks(dft_ref, spec, source)
+
+    def gather(hop, which):
+        transform(sources[which])
+        lag = 2 * hop
+
+        def body(base):
+            first, second = load_pair(spec, 0, base), load_pair(spec, 1, base)
+            here, after = load_pair(window_ref, lag, base), load_pair(window_ref, lag + 1, base)
+            one = product(first, here)
+            two = plus(product(first, after), product(second, here))
+            if hop == 0:
+                for block, value in ((0, one), (1, two)):
+                    total[block, pl.ds(base, ROWS_STEP), :] = value[0]
+                    total[block, pl.ds(BLOCK + base, ROWS_STEP), :] = value[1]
+            else:
+                one = plus(one, product(second, load_pair(window_ref, lag - 1, base)))
+                add_pair(total, 0, base, *one)
+                add_pair(total, 1, base, *two)
+
+        over_rows(body)
+
+    gather(0, 0)
+    each_hop(place_ref, False, gather)
+    for b in range(2):
+        parts = from_spectrum(inverse_ref, [total[b, rows, :] for rows in row_slices()])
+        for parity, result in enumerate(parts):
+            held = own[pl.ds(b * BLOCK + parity * HALF, HALF), :].astype(F32)
+            interleave(woven, b, parity, result + shift_ref[...] * held)
+    for side in range(TILE // 128):
+        lanes = pl.ds(side * 128, 128)
+        conv_ref[:, lanes] = woven[side].astype(BF16)
+        gated_ref[:, lanes] = (woven[side] * gate_ref[:, lanes].astype(F32)).astype(BF16)
+
+
+def conv_forward(place, own, partner, far, beyond, windows, dft, inverse, gate, shift):
+    rows, width = own.shape
+    tile = pl.BlockSpec((rows, TILE), lambda c, *_: (0, c))
+    return pl.pallas_call(
+        conv_forward_kernel,
+        grid_spec=pltpu.PrefetchScalarGridSpec(
+            num_scalar_prefetch=1,
+            grid=(width // TILE,),
+            in_specs=[tile] * 4
+            + [
+                pl.BlockSpec((windows.shape[0], 2 * BLOCK, TILE), lambda c, *_: (0, 0, c)),
+                pl.BlockSpec(dft.shape, lambda c, *_: (0, 0, 0)),
+                pl.BlockSpec(inverse.shape, lambda c, *_: (0, 0, 0)),
+                tile,
+                pl.BlockSpec((1, TILE), lambda c, *_: (0, c)),
+            ],
+            out_specs=[tile] * 2,
+            scratch_shapes=[
+                pltpu.VMEM((2, 2 * BLOCK, TILE), F32),
+                pltpu.VMEM((2, 2 * BLOCK, TILE), F32),
+                pltpu.VMEM((TILE // 128, rows, 128), F32),
+            ],
+        ),
+        out_shape=[jax.ShapeDtypeStruct((rows, width), BF16)] * 2,
+        compiler_params=pltpu.CompilerParams(vmem_limit_bytes=48 * MIB),
+        cost_estimate=LIGHT,
+        name="conv_forward",
+    )(place, own, partner, far, beyond, windows, dft, inverse, gate, shift)
+
+
+def conv_backward_kernel(
+    place_ref, own, partner, far, beyond, g_own, g_partner, g_far, g_beyond, window_ref, dft_ref, inverse_ref,
+    first, second, third, edge_one, edge_two, edge_three, taps_ref, shift_ref, g_gated_ref, conv_ref, rate_ref,
+    hidden_ref, last_ref, g_proj_ref, g_edge_ref, g_last_ref, g_middle_ref, g_taps_ref, g_shift_ref,
+    g_spec, spec, g_total, g_window, spread, woven,
+):
+    rows = own.shape[0]
+    count = g_window.shape[0] - 1
+
+    def transform(target, source):
+        transform_blocks(dft_ref, target, source)
+
+    g_sources = (g_own, g_partner, g_far, g_beyond)
+    sources = (own, partner, far, beyond)
+    g_total[...] = jnp.zeros_like(g_total)
+    g_window[...] = jnp.zeros_like(g_window)
+
+    def pull(hop, which):
+        lag = 2 * hop
+        held = g_spec
+        if hop > 0:
+            transform(spec, g_sources[which])
+            held = spec
+
+        def body(base):
+            one, two = load_pair(held, 0, base), load_pair(held, 1, base)
+            here, after = load_pair(window_ref, lag, base), load_pair(window_ref, lag + 1, base)
+            add_pair(g_total, 0, base, *plus(conj_product(here, one), conj_product(after, two)))
+            other = conj_product(here, two)
+            if hop > 0:
+                other = plus(other, conj_product(load_pair(window_ref, lag - 1, base), one))
+            add_pair(g_total, 1, base, *other)
+
+        over_rows(body)
+
+    def push(hop, which):
+        lag = 2 * hop
+        transform(spec, sources[which])
+
+        def body(base):
+            x_one, x_two = load_pair(spec, 0, base), load_pair(spec, 1, base)
+            one, two = load_pair(g_spec, 0, base), load_pair(g_spec, 1, base)
+            add_pair(g_window, lag, base, *plus(conj_product(x_one, one), conj_product(x_two, two)))
+            add_pair(g_window, lag + 1, base, *conj_product(x_one, two))
+            if hop > 0:
+                add_pair(g_window, lag - 1, base, *conj_product(x_two, one))
+
+        over_rows(body)
+
+    transform(g_spec, g_own)
+    pull(0, 0)
+    each_hop(place_ref, True, pull)
+    push(0, 0)
+    each_hop(place_ref, False, push)
+
+    stop = place_ref[3]
+    slowness = rate_ref[...] / place_ref[4].astype(F32)
+    last_bf = last_ref[...].astype(BF16)
+    table = spec.at[1, pl.ds(0, BLOCK)]
+    table[...] = jnp.exp(-block_offsets(0).astype(F32) * slowness)
+    g_last_ref[...] = jnp.zeros_like(g_last_ref)
+
+    @pl.when(pl.program_id(0) == 0)
+    def _():
+        g_middle_ref[...] = jnp.zeros_like(g_middle_ref)
+
+    for d in range(count):
+        @pl.when(d <= 2 * place_ref[0] + 1)
+        def _():
+            slices = row_slices()
+            sign = jnp.where(lax.broadcasted_iota(jnp.int32, (HALF, TILE), 0) < HALF // 2, 1.0, -1.0)
+            here = [g_window[d, rows, :] for rows in slices]
+            after = [g_window[d + 1, rows, :] for rows in slices]
+            parts = [
+                here[0] + sign * after[2], here[1] - sign * after[3],
+                here[2] - sign * after[0], here[3] + sign * after[1],
+            ]
+            lags = jnp.concatenate(from_spectrum(inverse_ref, parts), axis=0)
+            fade = jnp.exp(-float(d * BLOCK) * slowness)
+            g_raw = jnp.where(block_offsets(d) < stop, lags * (table[...] * fade), 0.0).astype(BF16)
+            at = pl.ds(d * BLOCK, BLOCK)
+            g_last_ref[...] += matmul(hidden_ref[:, at], g_raw)
+            g_middle_ref[at, :] += lax.dot_general(
+                g_raw, last_bf, (((1,), (1,)), ((), ())), preferred_element_type=F32
+            )
+
+    for b in range(2):
+        parts = from_spectrum(inverse_ref, [g_total[b, rows, :] for rows in row_slices()])
+        for parity, result in enumerate(parts):
+            held = g_own[pl.ds(b * BLOCK + parity * HALF, HALF), :].astype(F32)
+            interleave(woven, b, parity, result + shift_ref[...] * held)
+
+    for k, (source, edge) in enumerate(((first, edge_one), (second, edge_two), (third, edge_three))):
+        spread[k, pl.ds(0, EDGE), :] = edge[0].astype(F32)
+        spread[k, pl.ds(EDGE, rows), :] = source[...].astype(F32)
+    step = 32
+    g_taps_ref[...] = jnp.zeros_like(g_taps_ref)
+    g_shift_ref[...] = jnp.zeros_like(g_shift_ref)
+
+    def fold(values):
+        return jnp.sum(values.reshape(step // 8, 8, TILE), axis=0)
+
+    def shifts(k, base):
+        window = spread[k, pl.ds(pl.multiple_of(base + EDGE - 8, 8), step + 8), :]
+        return [window[8:]] + [pltpu.roll(window, lag, 0)[8:] for lag in (1, 2)]
+
+    def tapped(k, parts):
+        total = taps_ref[k : k + 1, :] * parts[0]
+        for lag in (1, 2):
+            total = total + taps_ref[3 * lag + k : 3 * lag + k + 1, :] * parts[lag]
+        return total
+
+    def one(index, carry):
+        base = pl.multiple_of(index * step, step)
+        at = pl.ds(base, step)
+        g_signal = jnp.concatenate([woven[side, at, :] for side in range(TILE // 128)], axis=1)
+        g_shift_ref[...] += fold(g_own[at, :].astype(F32) * own[at, :].astype(F32))
+        parts = shifts(0, base)
+        g_third = g_signal * tapped(0, parts)
+        more = shifts(2, base)
+        g_first = g_signal * tapped(2, more)
+        for lag in range(3):
+            g_taps_ref[3 * lag] += fold(g_first * parts[lag])
+            g_taps_ref[3 * lag + 2] += fold(g_third * more[lag])
+        g_window[0, at, :] = g_first
+        g_window[2, at, :] = g_third
+        g_second = g_gated_ref[at, :].astype(F32) * conv_ref[at, :].astype(F32)
+        parts = shifts(1, base)
+        for lag in range(3):
+            g_taps_ref[3 * lag + 1] += fold(g_second * parts[lag])
+        g_window[1, at, :] = g_second
+        return carry
+
+    lax.fori_loop(0, rows // step, one, 0, unroll=4)
+
+    for k in range(3):
+        g_edge_ref[k] = g_window[k, pl.ds(0, EDGE), :].astype(BF16)
+
+    def two(index, carry):
+        base = pl.multiple_of(index * step, step)
+        at = pl.ds(base, step)
+        for k in range(3):
+            window = spread[k, pl.ds(base, step + 8), :]
+            total = taps_ref[k : k + 1, :] * window[:step]
+            for lag in (1, 2):
+                moved = pltpu.roll(window, step + 8 - lag, 0)[:step]
+                total = total + taps_ref[3 * lag + k : 3 * lag + k + 1, :] * moved
+            g_proj_ref[k, at, :] = total.astype(BF16)
+        return carry
+
+    for k in range(3):
+        spread[k, pl.ds(0, rows), :] = g_window[k, pl.ds(0, rows), :]
+        spread[k, pl.ds(rows, EDGE), :] = jnp.zeros((EDGE, TILE), F32)
+    lax.fori_loop(0, rows // step, two, 0, unroll=4)
+
+
+def conv_backward(
+    place, signals, g_convs, windows, dft, inverse, projected, edge, taps, shift, g_gated, conv, rates, hidden, last
+):
+    rows, width = g_gated.shape
+    count = windows.shape[0]
+    tiles = width // TILE
+    tile = pl.BlockSpec((rows, TILE), lambda c, *_: (0, c))
+    line = pl.BlockSpec((1, TILE), lambda c, *_: (0, c))
+
+    def edge_at(k):
+        return lambda c, *_: (k, 0, c)
+
+    return pl.pallas_call(
+        conv_backward_kernel,
+        grid_spec=pltpu.PrefetchScalarGridSpec(
+            num_scalar_prefetch=1,
+            grid=(tiles,),
+            in_specs=[tile] * 8
+            + [
+                pl.BlockSpec((count, 2 * BLOCK, TILE), lambda c, *_: (0, 0, c)),
+                pl.BlockSpec(dft.shape, lambda c, *_: (0, 0, 0)),
+                pl.BlockSpec(inverse.shape, lambda c, *_: (0, 0, 0)),
+            ]
+            + [tile] * 3
+            + [pl.BlockSpec((1, EDGE, TILE), edge_at(k)) for k in range(3)]
+            + [
+                pl.BlockSpec((9, TILE), lambda c, *_: (0, c)), line, tile, tile, line,
+                pl.BlockSpec(hidden.shape, lambda c, *_: (0, 0)),
+                pl.BlockSpec((hidden.shape[0], TILE), lambda c, *_: (0, c)),
+            ],
+            out_specs=[
+                pl.BlockSpec((3, rows, TILE), lambda c, *_: (0, 0, c)),
+                pl.BlockSpec((3, EDGE, TILE), lambda c, *_: (0, 0, c)),
+                pl.BlockSpec((hidden.shape[0], TILE), lambda c, *_: (0, c)),
+                pl.BlockSpec((count * BLOCK, hidden.shape[0]), lambda c, *_: (0, 0)),
+                pl.BlockSpec((9, 8, TILE), lambda c, *_: (0, 0, c)),
+                pl.BlockSpec((8, TILE), lambda c, *_: (0, c)),
+            ],
+            scratch_shapes=[
+                pltpu.VMEM((2, 2 * BLOCK, TILE), F32),
+                pltpu.VMEM((2, 2 * BLOCK, TILE), F32),
+                pltpu.VMEM((2, 2 * BLOCK, TILE), F32),
+                pltpu.VMEM((count + 1, 2 * BLOCK, TILE), F32),
+                pltpu.VMEM((3, rows + EDGE, TILE), F32),
+                pltpu.VMEM((TILE // 128, rows, 128), F32),
+            ],
+        ),
+        out_shape=[
+            jax.ShapeDtypeStruct((3, rows, width), BF16),
+            jax.ShapeDtypeStruct((3, EDGE, width), BF16),
+            jax.ShapeDtypeStruct((hidden.shape[0], width), F32),
+            jax.ShapeDtypeStruct((count * BLOCK, hidden.shape[0]), F32),
+            jax.ShapeDtypeStruct((9, 8, width), F32),
+            jax.ShapeDtypeStruct((8, width), F32),
+        ],
+        compiler_params=pltpu.CompilerParams(vmem_limit_bytes=60 * MIB),
+        cost_estimate=LIGHT,
+        name="conv_backward",
+    )(
+        place, *signals, *g_convs, windows, dft, inverse, *projected,
+        edge, edge, edge, taps, shift, g_gated, conv, rates, hidden, last,
+    )
+
+
+PIECES = 2
+NEAR = (((1,), (1,)), ((), ()))
+LEAD = (((0,), (0,)), ((), ()))
+
+
+def matmul_near(left, right):
+    return lax.dot_general(left, right, NEAR, preferred_element_type=F32)
+
+
+def matmul_lead(left, right):
+    return lax.dot_general(left, right, LEAD, preferred_element_type=F32)
+
+
+def strip_of(z, c):
+    return pl.multiple_of((2 * z + c) * STRIP, STRIP)
+
+
+def start_columns(place_ref, pieces, which, target, sem, part):
+    z, c = place_ref[6], place_ref[7]
+    for dc in range(2):
+        own, others = pieces[dc * PIECES], pieces[dc * PIECES + 1]
+        to = target.at[pl.ds(strip_of(z, c ^ dc), STRIP), :]
+        pltpu.make_async_copy(own.at[part, which], to, sem).start()
+        for dz in range(1, 4):
+            to = target.at[pl.ds(strip_of(z ^ dz, c ^ dc), STRIP), :]
+            pltpu.make_async_copy(others.at[part, dz - 1, which], to, sem).start()
+
+
+def start_rows(place_ref, pieces, which, target, sem, line):
+    z, c = place_ref[6], place_ref[7]
+    dz = z ^ line
+    for dc in range(2):
+        own, others = pieces[dc * PIECES], pieces[dc * PIECES + 1]
+        for part in range(4):
+            row = pl.multiple_of((c ^ dc) * 4 * STRIP + part * STRIP, STRIP)
+            to = target.at[pl.ds(row, STRIP), :]
+
+            @pl.when(dz == 0)
+            def _():
+                pltpu.make_async_copy(own.at[part, which], to, sem).start()
+
+            @pl.when(dz > 0)
+            def _():
+                pltpu.make_async_copy(others.at[part, jnp.maximum(dz - 1, 0), which], to, sem).start()
+
+
+def wait_whole(target, sem):
+    pltpu.make_async_copy(target, target, sem).wait()
+
+
+def norm_rows(values, gain, bias):
+    average = jnp.mean(values, axis=-1, keepdims=True)
+    centred = values - average
+    variance = jnp.mean(centred * centred, axis=-1, keepdims=True)
+    return centred * lax.rsqrt(variance + 1e-05) * gain + bias
+
+
+def loop_rows(count, step, body, unroll=1):
+    def one(index, carry):
+        body(pl.multiple_of(index * step, step))
+        return carry
+
+    lax.fori_loop(0, count // step, one, 0, unroll=unroll)
+
+
+def part_rows(woven, first, target):
+    for side in range(woven.shape[0]):
+        for block in range(0, woven.shape[1], BLOCK):
+            for parity in range(2):
+                rows = woven[side, pl.ds(block + parity, HALF, stride=2), :]
+                at = pl.ds(first + block + parity * HALF, HALF)
+                target[at, pl.ds(side * 128, 128)] = rows.astype(BF16)
+
+
+def project_kernel(place_ref, stream, above, gain, bias, taps_ref, *rest):
+    pieces = rest[: 2 * PIECES]
+    normed_ref, one_ref, two_ref, three_ref, edge_ref, signal_ref, gate_ref, weights, held, spread, product_held, sem = rest[2 * PIECES :]
+    rows = stream.shape[0]
+    step_index = pl.program_id(0)
+
+    @pl.when(step_index == 0)
+    def _():
+        for part in range(3):
+            start_columns(place_ref, pieces, 0, weights.at[part], sem, part)
+
+        head = norm_rows(above[...], gain[...], bias[...])
+        held[pl.ds(0, EDGE), :] = jnp.where(place_ref[0] > 0, head, 0.0).astype(BF16)
+
+        def body(base):
+            values = norm_rows(stream[pl.ds(base, 128), :], gain[...], bias[...]).astype(BF16)
+            held[pl.ds(pl.multiple_of(EDGE + base, EDGE), 128), :] = values
+            normed_ref[pl.ds(base, 128), :] = values
+
+        loop_rows(rows, 128, body)
+        wait_whole(weights, sem)
+
+    tile_at = pl.ds(pl.multiple_of(step_index * TILE, TILE), TILE)
+    for k, ref in enumerate((one_ref, two_ref, three_ref)):
+        result = matmul(held[...], weights[k, :, tile_at]).astype(BF16)
+        ref[...] = result[EDGE:]
+        edge_ref[k] = result[:EDGE]
+        spread[k] = result.astype(F32)
+
+    def body(base):
+        mixed = []
+        for k in range(3):
+            window = spread[k, pl.ds(pl.multiple_of(base + EDGE - 8, 8), 40), :]
+            total = taps_ref[k : k + 1, :] * window[8:]
+            for lag in (1, 2):
+                moved = pltpu.roll(window, lag, 0)[8:]
+                total = total + taps_ref[3 * lag + k : 3 * lag + k + 1, :] * moved
+            mixed.append(total)
+        at = pl.ds(base, 32)
+        signal = mixed[0] * mixed[2]
+        for side in range(TILE // 128):
+            product_held[side, at, :] = signal[:, side * 128 : side * 128 + 128]
+        gate_ref[at, :] = mixed[1].astype(BF16)
+
+    loop_rows(rows, 32, body, unroll=8)
+    part_rows(product_held, 0, signal_ref)
+
+
+def once(shape):
+    zeros = (0,) * len(shape)
+    return pl.BlockSpec(shape, lambda *_: zeros, pipeline_mode=pl.Buffered(1))
+
+
+ANYWHERE = pl.BlockSpec(memory_space=pl.ANY)
+
+
+def project(place, stream, above, gain, bias, taps, pieces):
+    rows, width = stream.shape
+    tile = pl.BlockSpec((rows, TILE), lambda c, *_: (0, c))
+    return pl.pallas_call(
+        project_kernel,
+        grid_spec=pltpu.PrefetchScalarGridSpec(
+            num_scalar_prefetch=1,
+            grid=(width // TILE,),
+            in_specs=[
+                once((rows, width)), once((EDGE, width)), once((1, width)), once((1, width)),
+                pl.BlockSpec((9, TILE), lambda c, *_: (0, c)),
+            ]
+            + [ANYWHERE] * (2 * PIECES),
+            out_specs=[once((rows, width)), tile, tile, tile,
+                       pl.BlockSpec((3, EDGE, TILE), lambda c, *_: (0, 0, c)), tile, tile],
+            scratch_shapes=[
+                pltpu.VMEM((3, width, width), BF16),
+                pltpu.VMEM((rows + EDGE, width), BF16),
+                pltpu.VMEM((3, rows + EDGE, TILE), F32),
+                pltpu.VMEM((TILE // 128, rows, 128), F32),
+                pltpu.SemaphoreType.DMA,
+            ],
+        ),
+        out_shape=[jax.ShapeDtypeStruct((rows, width), BF16)] * 4
+        + [jax.ShapeDtypeStruct((3, EDGE, width), BF16)]
+        + [jax.ShapeDtypeStruct((rows, width), BF16)] * 2,
+        compiler_params=pltpu.CompilerParams(vmem_limit_bytes=48 * MIB),
+        cost_estimate=LIGHT,
+        name="project",
+    )(place, stream, above, gain, bias, taps, *pieces)
+
+
+def gelu_and_slope(values):
+    size = jnp.abs(values)
+    bell = jnp.exp(-0.5 * values * values)
+    t = pl.reciprocal(1.0 + (0.3275911 * math.sqrt(0.5)) * size)
+    tail = 0.5 * 1.061405429 * t + 0.5 * -1.453152027
+    tail = tail * t + 0.5 * 1.421413741
+    tail = tail * t + 0.5 * -0.284496736
+    tail = tail * t + 0.5 * 0.254829592
+    tail = tail * t * bell
+    below = jnp.where(values < 0.0, tail, 1.0 - tail)
+    return values * below, below + values * bell * (1.0 / math.sqrt(2.0 * math.pi))
+
+
+def feed_kernel(place_ref, stream, gated, gain, bias, *rest):
+    mixer_pieces, feed_pieces = rest[: 2 * PIECES], rest[2 * PIECES : 4 * PIECES]
+    (out_ref, middle_ref, normed_ref, hidden_ref, slope_ref, w_out, w_up, w_down,
+     out_sem, up_sem, down_sem) = rest[4 * PIECES :]
+    rows = stream.shape[0]
+    step_index = pl.program_id(0)
+    slot = step_index % 2
+
+    def fetch(part):
+        start_columns(place_ref, feed_pieces, 0, w_up.at[part % 2], up_sem.at[part % 2], part)
+        start_rows(place_ref, feed_pieces, 1, w_down.at[part % 2], down_sem.at[part % 2], part)
+
+    @pl.when(step_index == 0)
+    def _():
+        start_columns(place_ref, mixer_pieces, 0, w_out, out_sem, 3)
+        fetch(0)
+        wait_whole(w_out, out_sem)
+
+        def body(base):
+            at = pl.ds(base, 512)
+            middle_ref[at, :] = stream[at, :] + matmul(gated[at, :], w_out[...])
+
+        loop_rows(rows, 512, body)
+
+        def norm(base):
+            at = pl.ds(base, 128)
+            middle = middle_ref[at, :]
+            out_ref[at, :] = middle
+            normed_ref[at, :] = norm_rows(middle, gain[...], bias[...]).astype(BF16)
+
+        loop_rows(rows, 128, norm)
+
+    for part in range(1, 4):
+        @pl.when(step_index == part - 1)
+        def _():
+            fetch(part)
+
+    wait_whole(w_up.at[slot], up_sem.at[slot])
+    wait_whole(w_down.at[slot], down_sem.at[slot])
+
+    def body(base):
+        at = pl.ds(base, 512)
+        pre_act = matmul(normed_ref[at, :], w_up[slot])
+        hidden, slope = gelu_and_slope(pre_act)
+        hidden = hidden.astype(BF16)
+        hidden_ref[at, :] = hidden
+        slope_ref[at, :] = slope.astype(BF16)
+        out_ref[at, :] += matmul(hidden, w_down[slot])
+
+    loop_rows(rows, 512, body)
+
+
+def feed_forward(place, stream, gated, gain, bias, mixer_pieces, feed_pieces):
+    rows, width = stream.shape
+    part = pl.BlockSpec((rows, width), lambda j, *_: (0, j))
+    return pl.pallas_call(
+        feed_kernel,
+        grid_spec=pltpu.PrefetchScalarGridSpec(
+            num_scalar_prefetch=1,
+            grid=(4,),
+            in_specs=[once((rows, width)), once((rows, width)), once((1, width)), once((1, width))]
+            + [ANYWHERE] * (4 * PIECES),
+            out_specs=[once((rows, width)), once((rows, width)), once((rows, width)), part, part],
+            scratch_shapes=[
+                pltpu.VMEM((width, width), BF16),
+                pltpu.VMEM((2, width, width), BF16),
+                pltpu.VMEM((2, width, width), BF16),
+                pltpu.SemaphoreType.DMA,
+                pltpu.SemaphoreType.DMA((2,)),
+                pltpu.SemaphoreType.DMA((2,)),
+            ],
+        ),
+        out_shape=[
+            jax.ShapeDtypeStruct((rows, width), F32),
+            jax.ShapeDtypeStruct((rows, width), F32),
+            jax.ShapeDtypeStruct((rows, width), BF16),
+            jax.ShapeDtypeStruct((rows, 4 * width), BF16),
+            jax.ShapeDtypeStruct((rows, 4 * width), BF16),
+        ],
+        compiler_params=pltpu.CompilerParams(vmem_limit_bytes=56 * MIB),
+        cost_estimate=LIGHT,
+        name="feed_forward",
+    )(place, stream, gated, gain, bias, *mixer_pieces, *feed_pieces)
+
+
+def norm_backward(values, g_normed, gain):
+    average = jnp.mean(values, axis=-1, keepdims=True)
+    centred = values - average
+    variance = jnp.mean(centred * centred, axis=-1, keepdims=True)
+    scale = lax.rsqrt(variance + 1e-05)
+    unit = centred * scale
+    g_unit = g_normed * gain
+    inner = g_unit - jnp.mean(g_unit, axis=-1, keepdims=True)
+    inner = inner - unit * jnp.mean(g_unit * unit, axis=-1, keepdims=True)
+    return inner * scale, g_normed * unit
+
+
+def fold_rows(values):
+    return jnp.sum(values.reshape(values.shape[0] // 8, 8, values.shape[1]), axis=0)
+
+
+def feed_backward_kernel(place_ref, g_stream, middle, gain, gate, slope_ref, *rest):
+    mixer_pieces, feed_pieces = rest[: 2 * PIECES], rest[2 * PIECES : 4 * PIECES]
+    (g_down_ref, g_pre_ref, g_mid_ref, g_out_ref, g_gated_ref, g_conv_ref, g_gain_ref, g_bias_ref,
+     w_out, w_up, w_down, total, woven, out_sem, up_sem, down_sem) = rest[4 * PIECES :]
+    rows = g_stream.shape[0]
+    step_index = pl.program_id(0)
+    slot = step_index % 2
+
+    def fetch(part):
+        start_columns(place_ref, feed_pieces, 0, w_up.at[part % 2], up_sem.at[part % 2], part)
+        start_rows(place_ref, feed_pieces, 1, w_down.at[part % 2], down_sem.at[part % 2], part)
+
+    @pl.when(step_index == 0)
+    def _():
+        fetch(0)
+        start_columns(place_ref, mixer_pieces, 0, w_out, out_sem, 3)
+        g_down_ref[...] = g_stream[...].astype(BF16)
+        total[...] = jnp.zeros_like(total)
+
+    for part in range(1, 4):
+        @pl.when(step_index == part - 1)
+        def _():
+            fetch(part)
+
+    wait_whole(w_up.at[slot], up_sem.at[slot])
+    wait_whole(w_down.at[slot], down_sem.at[slot])
+
+    def body(base):
+        at = pl.ds(base, 512)
+        g_hidden = matmul_near(g_down_ref[at, :], w_down[slot])
+        g_pre = (g_hidden * slope_ref[at, :].astype(F32)).astype(BF16)
+        g_pre_ref[at, :] = g_pre
+        total[at, :] += matmul_near(g_pre, w_up[slot])
+
+    loop_rows(rows, 512, body)
+
+    @pl.when(step_index == 3)
+    def _():
+        wait_whole(w_out, out_sem)
+        g_gain_ref[...] = jnp.zeros_like(g_gain_ref)
+        g_bias_ref[...] = jnp.zeros_like(g_bias_ref)
+
+        def last(base):
+            at = pl.ds(base, 128)
+            g_normed = total[at, :]
+            g_value, g_scaled = norm_backward(middle[at, :], g_normed, gain[...])
+            g_mid = g_stream[at, :] + g_value
+            g_mid_ref[at, :] = g_mid
+            g_out_ref[at, :] = g_mid.astype(BF16)
+            g_gain_ref[...] += fold_rows(g_scaled)
+            g_bias_ref[...] += fold_rows(g_normed)
+
+        loop_rows(rows, 128, last)
+
+        for first in range(0, rows, BLOCK):
+            at = pl.ds(first, BLOCK)
+            g_gated = matmul_near(g_out_ref[at, :], w_out[...]).astype(BF16)
+            g_gated_ref[at, :] = g_gated
+            g_conv = g_gated.astype(F32) * gate[at, :].astype(F32)
+            for side in range(woven.shape[0]):
+                woven[side] = g_conv[:, side * 128 : side * 128 + 128]
+            part_rows(woven, first, g_conv_ref)
+
+
+def feed_backward(place, g_stream, middle, gain, gate, slope, mixer_pieces, feed_pieces):
+    rows, width = g_stream.shape
+    part = pl.BlockSpec((rows, width), lambda j, *_: (0, j))
+    whole = once((rows, width))
+    return pl.pallas_call(
+        feed_backward_kernel,
+        grid_spec=pltpu.PrefetchScalarGridSpec(
+            num_scalar_prefetch=1,
+            grid=(4,),
+            in_specs=[whole, whole, once((1, width)), whole, part] + [ANYWHERE] * (4 * PIECES),
+            out_specs=[whole, part, whole, whole, whole, whole, once((8, width)), once((8, width))],
+            scratch_shapes=[
+                pltpu.VMEM((width, width), BF16),
+                pltpu.VMEM((2, width, width), BF16),
+                pltpu.VMEM((2, width, width), BF16),
+                pltpu.VMEM((rows, width), F32),
+                pltpu.VMEM((width // 128, BLOCK, 128), F32),
+                pltpu.SemaphoreType.DMA,
+                pltpu.SemaphoreType.DMA((2,)),
+                pltpu.SemaphoreType.DMA((2,)),
+            ],
+        ),
+        out_shape=[
+            jax.ShapeDtypeStruct((rows, width), BF16),
+            jax.ShapeDtypeStruct((rows, 4 * width), BF16),
+            jax.ShapeDtypeStruct((rows, width), F32),
+            jax.ShapeDtypeStruct((rows, width), BF16),
+            jax.ShapeDtypeStruct((rows, width), BF16),
+            jax.ShapeDtypeStruct((rows, width), BF16),
+            jax.ShapeDtypeStruct((8, width), F32),
+            jax.ShapeDtypeStruct((8, width), F32),
+        ],
+        compiler_params=pltpu.CompilerParams(vmem_limit_bytes=58 * MIB),
+        cost_estimate=LIGHT,
+        name="feed_backward",
+    )(place, g_stream, middle, gain, gate, slope, *mixer_pieces, *feed_pieces)
+
+
+def project_backward_kernel(place_ref, g_proj, stream, g_mid, gain, *rest):
+    pieces = rest[: 2 * PIECES]
+    g_stream_ref, g_gain_ref, g_bias_ref, weights, total, sem = rest[2 * PIECES :]
+    rows = stream.shape[0]
+    for part in range(3):
+        start_columns(place_ref, pieces, 0, weights.at[part], sem, part)
+    wait_whole(weights, sem)
+    g_gain_ref[...] = jnp.zeros_like(g_gain_ref)
+    g_bias_ref[...] = jnp.zeros_like(g_bias_ref)
+
+    total[...] = matmul_near(g_proj[0], weights[0])
+    total[...] += matmul_near(g_proj[1], weights[1])
+    total[...] += matmul_near(g_proj[2], weights[2])
+
+    def last(base):
+        at = pl.ds(base, 128)
+        g_normed = total[at, :]
+        g_value, g_scaled = norm_backward(stream[at, :], g_normed, gain[...])
+        g_stream_ref[at, :] = g_mid[at, :] + g_value
+        g_gain_ref[...] += fold_rows(g_scaled)
+        g_bias_ref[...] += fold_rows(g_normed)
+
+    loop_rows(rows, 128, last)
+
+
+def project_backward(place, g_proj, stream, g_mid, gain, pieces):
+    rows, width = stream.shape
+    whole = once((rows, width))
+    return pl.pallas_call(
+        project_backward_kernel,
+        grid_spec=pltpu.PrefetchScalarGridSpec(
+            num_scalar_prefetch=1,
+            grid=(1,),
+            in_specs=[once((3, rows, width)), whole, whole, once((1, width))] + [ANYWHERE] * (2 * PIECES),
+            out_specs=[whole, once((8, width)), once((8, width))],
+            scratch_shapes=[
+                pltpu.VMEM((3, width, width), BF16),
+                pltpu.VMEM((rows, width), F32),
+                pltpu.SemaphoreType.DMA,
+            ],
+        ),
+        out_shape=[
+            jax.ShapeDtypeStruct((rows, width), F32),
+            jax.ShapeDtypeStruct((8, width), F32),
+            jax.ShapeDtypeStruct((8, width), F32),
+        ],
+        compiler_params=pltpu.CompilerParams(vmem_limit_bytes=48 * MIB),
+        cost_estimate=LIGHT,
+        name="project_backward",
+    )(place, g_proj, stream, g_mid, gain, *pieces)
+
+
+def strip_at(hold, z, c):
+    return hold[pl.ds(strip_of(z, c), STRIP), :].astype(BF16)
+
+
+def grad_up_kernel(place_ref, normed, g_pre, keep_ref, send_ref, hold):
+    c = place_ref[7]
+    hold[...] = matmul_lead(normed[...], g_pre[...])
+    for z in range(4):
+        keep_ref[0, z] = strip_at(hold, z, c)
+        send_ref[0, z] = strip_at(hold, z, c ^ 1)
+
+
+def grad_up(place, normed, g_pre):
+    rows, width = normed.shape
+    part = pl.BlockSpec((rows, width), lambda j, *_: (0, j))
+    block = pl.BlockSpec((1, 4, STRIP, width), lambda j, *_: (j, 0, 0, 0))
+    return pl.pallas_call(
+        grad_up_kernel,
+        grid_spec=pltpu.PrefetchScalarGridSpec(
+            num_scalar_prefetch=1,
+            grid=(4,),
+            in_specs=[once((rows, width)), part],
+            out_specs=[block, block],
+            scratch_shapes=[pltpu.VMEM((width, width), F32)],
+        ),
+        out_shape=[jax.ShapeDtypeStruct((4, 4, STRIP, width), BF16)] * 2,
+        compiler_params=pltpu.CompilerParams(vmem_limit_bytes=40 * MIB),
+        cost_estimate=LIGHT,
+        name="grad_up",
+    )(place, normed, g_pre)
+
+
+def grad_down_kernel(place_ref, hidden, g_down, keep_ref, send_ref, hold):
+    c = place_ref[7]
+    hold[...] = matmul_lead(hidden[...], g_down[...])
+    for part in range(4):
+        for ref, side in ((keep_ref, c), (send_ref, c ^ 1)):
+            row = pl.multiple_of((side * 4 + part) * STRIP, STRIP)
+            ref[part, 0] = hold[pl.ds(row, STRIP), :].astype(BF16)
+
+
+def grad_down(place, hidden, g_down):
+    rows, width = g_down.shape
+    block = pl.BlockSpec((4, 1, STRIP, width), lambda j, *_: (0, j, 0, 0))
+    return pl.pallas_call(
+        grad_down_kernel,
+        grid_spec=pltpu.PrefetchScalarGridSpec(
+            num_scalar_prefetch=1,
+            grid=(4,),
+            in_specs=[pl.BlockSpec((rows, width), lambda j, *_: (0, j)), once((rows, width))],
+            out_specs=[block, block],
+            scratch_shapes=[pltpu.VMEM((width, width), F32)],
+        ),
+        out_shape=[jax.ShapeDtypeStruct((4, 4, STRIP, width), BF16)] * 2,
+        compiler_params=pltpu.CompilerParams(vmem_limit_bytes=40 * MIB),
+        cost_estimate=LIGHT,
+        name="grad_down",
+    )(place, hidden, g_down)
+
+
+def grad_rows_kernel(place_ref, left, right, keep_ref, send_ref, hold):
+    c = place_ref[7]
+    quarter = STRIP // 4
+    hold[...] = matmul_lead(left[...], right[0])
+    for z in range(4):
+        for ref, side in ((keep_ref, c), (send_ref, c ^ 1)):
+            for part in range(4):
+                row = pl.multiple_of(strip_of(z, side) + part * quarter, quarter)
+                ref[part, z, 0] = hold[pl.ds(row, quarter), :].astype(BF16)
+
+
+def grad_rows(place, left, right):
+    count, rows, width = right.shape
+    block = pl.BlockSpec((4, 4, 1, STRIP // 4, width), lambda j, *_: (0, 0, j, 0, 0))
+    return pl.pallas_call(
+        grad_rows_kernel,
+        grid_spec=pltpu.PrefetchScalarGridSpec(
+            num_scalar_prefetch=1,
+            grid=(count,),
+            in_specs=[once((rows, width)), pl.BlockSpec((1, rows, width), lambda j, *_: (j, 0, 0))],
+            out_specs=[block, block],
+            scratch_shapes=[pltpu.VMEM((width, width), F32)],
+        ),
+        out_shape=[jax.ShapeDtypeStruct((4, 4, count, STRIP // 4, width), BF16)] * 2,
+        compiler_params=pltpu.CompilerParams(vmem_limit_bytes=40 * MIB),
+        cost_estimate=LIGHT,
+        name="grad_rows",
+    )(place, left, right)
+
+
+def order_kernel(place_ref, held_ref, out_ref):
+    out_ref[...] = held_ref[0]
+
+
+def in_channel_order(place, held):
+    count, rows, width = held.shape
+    return pl.pallas_call(
+        order_kernel,
+        grid_spec=pltpu.PrefetchScalarGridSpec(
+            num_scalar_prefetch=1,
+            grid=(count,),
+            in_specs=[pl.BlockSpec((1, rows, width), lambda j, *_: (j, 0, 0))],
+            out_specs=pl.BlockSpec((rows, width), lambda j, place_ref: (0, j ^ (2 * place_ref[6] + place_ref[7]))),
+        ),
+        out_shape=jax.ShapeDtypeStruct((rows, count * width), F32),
+        cost_estimate=LIGHT,
+        name="in_channel_order",
+    )(place, held)
+
+
+def lay_out_kernel(place_ref, ones, zero, near, side, cross, up_ref, down_ref, out_ref, in_ref):
+    width = down_ref.shape[2]
+    quarter = STRIP // 4
+    s = place_ref[5]
+
+    def lay(layer, part, sums):
+        up_ref[layer, :, pl.ds(part * width, width)] = sums[:STRIP].astype(F32)
+        down_ref[layer, pl.ds(part * STRIP, STRIP), :] = sums[STRIP : 2 * STRIP].astype(F32)
+        rows = pl.ds(part * quarter, quarter)
+        out_ref[layer, rows, :] = sums[2 * STRIP : 2 * STRIP + quarter].astype(F32)
+        for k in range(3):
+            first = 2 * STRIP + (k + 1) * quarter
+            in_ref[layer, rows, pl.ds(k * width, width)] = sums[first : first + quarter].astype(F32)
+
+    for part in range(4):
+        lay(1, part, ones[part])
+        for hop, source in enumerate((zero, near, side, cross)):
+            pl.when((s ^ hop) == part)(functools.partial(lambda p, r: lay(0, p, r[...]), part, source))
+
+
+def lay_out(place, ones, zeros):
+    width = ones.shape[2]
+    shapes = [(2, STRIP, 4 * width), (2, 4 * STRIP, width), (2, STRIP, width), (2, STRIP, 3 * width)]
+    return pl.pallas_call(
+        lay_out_kernel,
+        grid_spec=pltpu.PrefetchScalarGridSpec(
+            num_scalar_prefetch=1,
+            grid=(1,),
+            in_specs=[once(ones.shape)] + [once(zeros[0].shape)] * 4,
+            out_specs=[once(shape) for shape in shapes],
+        ),
+        out_shape=[jax.ShapeDtypeStruct(shape, F32) for shape in shapes],
+        compiler_params=pltpu.CompilerParams(vmem_limit_bytes=40 * MIB),
+        cost_estimate=LIGHT,
+        name="lay_out",
+    )(place, ones, *zeros)
+
+
+FIRST_STEPS = (((0, 2), (1, 3)), ((0, 1), (2, 3)))
+
+
+def merge_kernel(place_ref, *refs, count, form):
+    keeps, gots, outs = refs[:count], refs[count : 2 * count], refs[2 * count :]
+    s = place_ref[5]
+    for part in range(4):
+        at = part if form == "whole" else s ^ part
+        rows = [
+            (keep[at, 0].astype(F32) + got[at, 0].astype(F32)).astype(BF16) for keep, got in zip(keeps, gots)
+        ]
+        rows = jnp.concatenate(rows, axis=0) if count > 1 else rows[0]
+        if form == "whole":
+            outs[0][part, 0] = rows
+        elif form == "hops":
+            outs[part][0] = rows
+        else:
+            half = rows.shape[0] // 2
+            for side, groups in enumerate(FIRST_STEPS):
+                for group, hops in enumerate(groups):
+                    if part in hops:
+                        outs[2 * side + group][hops.index(part), 0] = rows[side * half : side * half + half]
+
+
+def merge_cores(place, keeps, gots, form):
+    width = keeps[0].shape[-1]
+    rows = sum(keep.shape[2] for keep in keeps)
+    blocks = [pl.BlockSpec((4, 1, keep.shape[2], width), lambda j, *_: (0, j, 0, 0)) for keep in keeps]
+    if form == "hops":
+        out_specs = [pl.BlockSpec((1, rows, width), lambda j, *_: (j, 0, 0))] * 4
+        out_shape = [jax.ShapeDtypeStruct((4, rows, width), BF16)] * 4
+    elif form == "whole":
+        out_specs = [pl.BlockSpec((4, 1, rows, width), lambda j, *_: (0, j, 0, 0))]
+        out_shape = [jax.ShapeDtypeStruct((4, 4, rows, width), BF16)]
+    else:
+        out_specs = [pl.BlockSpec((2, 1, rows // 2, width), lambda j, *_: (0, j, 0, 0))] * 4
+        out_shape = [jax.ShapeDtypeStruct((2, 4, rows // 2, width), BF16)] * 4
+    return pl.pallas_call(
+        functools.partial(merge_kernel, count=len(keeps), form=form),
+        grid_spec=pltpu.PrefetchScalarGridSpec(
+            num_scalar_prefetch=1, grid=(4,), in_specs=blocks * 2, out_specs=out_specs
+        ),
+        out_shape=out_shape,
+        compiler_params=pltpu.CompilerParams(vmem_limit_bytes=40 * MIB),
+        cost_estimate=LIGHT,
+        name="merge_cores",
+    )(place, *keeps, *gots)
+
+
+def xor_pairs(count, bits):
+    return [(i, i ^ bits) for i in range(count)]
+
+
+def hop_pairs(chan_count, per_group, shift):
+    return [
+        (i, i + shift)
+        for i in range(chan_count)
+        if 0 <= i % per_group + shift < per_group
+    ]
+
+
+def across_cores(values):
+    return lax.ppermute(values, "core", xor_pairs(lax.axis_size("core"), 1))
+
+
+def across_line(values, hop):
+    return lax.ppermute(values, "line", xor_pairs(lax.axis_size("line"), hop))
+
+
+def across_plane(values, hop):
+    return lax.ppermute(values, "seq", xor_pairs(lax.axis_size("seq"), hop))
+
+
+def pick(values, index):
+    return lax.dynamic_index_in_dim(values, index, axis=0, keepdims=False)
+
+
+def barrier(*values):
+    return lax.optimization_barrier(values)
+
+
+def line_pieces(shard, s):
+    mine = pick(shard, s)
+    return [across_line(mine, hop) for hop in range(1, 4)]
+
+
+def to_planes(values, hops=(1, 2, 3)):
+    return [across_plane(values, hop) for hop in hops]
+
+
+def in_order(held, s):
+    held = jnp.stack(held)
+    return jnp.stack([pick(held, s ^ part) for part in range(4)])
+
+
+def add_all(first, others):
+    total = first.astype(F32)
+    for values in others:
+        total = total + values.astype(F32)
+    return total.astype(BF16)
+
+
+def send_planes(parts):
+    return [across_plane(parts[hop], hop) for hop in range(1, 4)]
+
+
+def send_lines(values, z, hops=(1, 2, 3)):
+    return [across_line(pick(values, z ^ hop), hop) for hop in hops]
+
+
+def scatter_planes(values):
+    return lax.psum_scatter(values, "seq", scatter_dimension=0, tiled=False)
+
+
+def scatter_lines(values):
+    return lax.psum_scatter(values, "line", scatter_dimension=0, tiled=False)
+
+
+def share_planes(values):
+    return lax.all_gather(values, "seq", axis=0)
+
+
+def sum_everywhere(values):
+    for send in (
+        across_cores,
+        lambda v: across_line(v, 1),
+        lambda v: across_line(v, 2),
+        lambda v: across_plane(v, 1),
+        lambda v: across_plane(v, 2),
+    ):
+        values = values + send(values)
+    return values
+
+
+def gather_small(values):
+    held = values[None]
+    for send in (across_cores, lambda v: across_line(v, 1), lambda v: across_line(v, 2)):
+        held = jnp.concatenate([held, send(held)], axis=0)
+    return held
+
+
+def chan_permute(values, pairs):
+    return lax.ppermute(values, ("line", "core"), pairs)
+
+
+def sequence_local(
+    tokens_in,
+    ln_gain,
+    ln_bias,
+    in_weight,
+    short_weight,
+    filter_first,
+    filter_mid,
+    filter_last,
+    conv_bias,
+    out_weight,
+    up_weight,
+    down_weight,
+    group_kind,
+    filt_len,
+    decay_win,
+    cotangent,
+):
+    chan_count = lax.axis_size("line") * lax.axis_size("core")
+    seq_index = lax.axis_index("seq")
+    chan_index = lax.axis_index(("line", "core"))
+    local_rows, width = tokens_in.shape
+    chan_width = conv_bias.shape[1]
+    hid = filter_last.shape[1]
+    per_group = chan_count // 2
+    group_len = local_rows * per_group
+    place_in = chan_index % per_group
+    line_index = chan_index // 2
+    group_index = 2 * seq_index + chan_index // per_group
+    kind = pick(group_kind, group_index)
+    stop = pick(filt_len, group_index)
+    span = pick(decay_win, group_index)
+    earlier = jnp.where(kind == 1, place_in, place_in % 2)
+    later = jnp.where(kind == 1, per_group - 1 - place_in, 1 - place_in % 2)
+    place = jnp.stack(
+        [earlier, later, place_in % 2, stop, span, seq_index, line_index, chan_index % 2]
+    ).astype(jnp.int32)
+    dft, inverse = (jnp.asarray(table) for table in transform_tables())
+    rates = jnp.exp(
+        jnp.log(0.3) + jnp.log(100.0) * jnp.arange(width, dtype=jnp.int32).astype(F32) / (width - 1)
+    )[None, :]
+    row = jnp.arange(group_len, dtype=jnp.int32)
+    positions = (row // BLOCK * BLOCK + row % HALF * 2 + row % BLOCK // HALF).astype(F32)
+    features = position_features(positions, group_len)
+    ahead = hop_pairs(chan_count, per_group, 2)
+    back = hop_pairs(chan_count, per_group, -2)
+    ahead_one = hop_pairs(chan_count, per_group, 1)
+    back_one = hop_pairs(chan_count, per_group, -1)
+
+    def neighbours(values, pairs):
+        partner = across_cores(values)
+        far = chan_permute(values, pairs)
+        return (values, partner, far, across_cores(far))
+
+    small = jnp.concatenate(
+        [
+            filter_last,
+            short_weight.reshape(LAYERS, 9, chan_width),
+            conv_bias[:, None, :],
+            ln_gain.astype(F32),
+            ln_bias.astype(F32),
+        ],
+        axis=1,
+    )
+
+    def mixer_shard(layer_index):
+        columns = in_weight[layer_index].reshape(chan_width, 3, width).transpose(1, 0, 2)
+        return jnp.concatenate([columns, out_weight[layer_index][None]])[:, None]
+
+    def feed_shard(layer_index):
+        up = up_weight[layer_index].reshape(chan_width, 4, width).transpose(1, 0, 2)
+        down = down_weight[layer_index].reshape(4, chan_width, width)
+        return jnp.stack([up, down], axis=1)
+
+    def filter_acts(layer_index):
+        first_act = precise_dot(features, filter_first[layer_index])
+        first_sin = jnp.sin(first_act)
+        middle_act = precise_dot(first_sin, filter_mid[layer_index])
+        middle_sin = jnp.sin(middle_act)
+        high = middle_sin.astype(BF16)
+        low = (middle_sin - high.astype(F32)).astype(BF16)
+        return first_act, first_sin, middle_act, jnp.concatenate([high, high, low], axis=1), high.T
+
+    mixer_shards = [mixer_shard(layer_index) for layer_index in range(LAYERS)]
+    feed_shards = [feed_shard(layer_index) for layer_index in range(LAYERS)]
+    s, z = seq_index, line_index
+
+    def line_hops(shard, hops):
+        mine = pick(shard, s)
+        return [across_line(mine, hop) for hop in hops]
+
+    mixer_line = line_pieces(mixer_shards[0], s)
+    feed_line = line_hops(feed_shards[0], (1,))
+    mixer_line, feed_line, feed_shards[0], filter_first = barrier(mixer_line, feed_line, feed_shards[0], filter_first)
+
+    windows = [None] * LAYERS
+    small = gather_small(small.reshape(-1, chan_width))
+    mixer_line = jnp.stack(mixer_line)
+    mixer_plane = to_planes(mixer_line)
+    feed_line = feed_line + line_hops(feed_shards[0], (2,))
+    acts = [filter_acts(layer_index) for layer_index in range(LAYERS)]
+    mixer_line, mixer_plane, small, acts, feed_line, place = barrier(
+        mixer_line, mixer_plane, small, acts, feed_line, place
+    )
+
+    mixer_pieces, feed_pieces = [None] * LAYERS, [None] * LAYERS
+    mixer_all = in_order([mixer_line, *mixer_plane], s)
+    mixer_all_twin = across_cores(mixer_all)
+    mixer_twin = across_cores(mixer_shards[0])
+    above = chan_permute(tokens_in[-EDGE:], ahead_one)
+    feed_line = feed_line + line_hops(feed_shards[0], (3,))
+    small = in_channel_order(place, small).reshape(LAYERS, hid + 14, width)
+    mixer_all, mixer_all_twin, mixer_twin, above, small, feed_line = barrier(
+        mixer_all, mixer_all_twin, mixer_twin, above, small, feed_line
+    )
+    mixer_pieces[0] = [mixer_shards[0], mixer_all, mixer_twin, mixer_all_twin]
+    last_all, taps_all, shift_all = small[:, :hid], small[:, hid : hid + 9], small[:, hid + 9 : hid + 10]
+    gain_all, bias_all = small[:, hid + 10 : hid + 12], small[:, hid + 12 : hid + 14]
+
+    def last_parts(i):
+        high = last_all[i].astype(BF16)
+        low = (last_all[i] - high.astype(F32)).astype(BF16)
+        return jnp.concatenate([high, low, high], axis=0)
+
+    stream = tokens_in
+    kept = []
+    for i in range(LAYERS):
+        more = i + 1 < LAYERS
+        if more:
+            twins = [across_cores(v) for v in (feed_shards[0], mixer_shards[1])]
+            feed_line = jnp.stack(feed_line)
+            feed_plane = to_planes(feed_line, (1, 2))
+        normed_in, *projected, edge, signal, gate = project(
+            place, stream, above, gain_all[i, :1], bias_all[i, :1], taps_all[i], mixer_pieces[i]
+        )
+        if more:
+            signal, projected, feed_line, feed_plane, twins = barrier(signal, projected, feed_line, feed_plane, twins)
+        else:
+            signal, projected = barrier(signal, projected)
+        partner = across_cores(signal)
+        far = chan_permute(signal, ahead)
+        if more:
+            feed_plane = feed_plane + to_planes(feed_line, (3,))
+        windows[i] = window_spectra(place, acts[i][3], last_parts(i), rates, dft)
+        if more:
+            far, partner, feed_plane, windows[i] = barrier(far, partner, feed_plane, windows[i])
+            feed_all = in_order([feed_line, *feed_plane], s)
+        else:
+            cosines = [(jnp.cos(acts[0][0]), jnp.cos(acts[0][2])), None]
+            far, partner, feed_all, windows[i], cosines[0] = barrier(far, partner, feed_all, windows[i], cosines[0])
+        beyond = across_cores(far)
+        feed_all_twin = across_cores(feed_all)
+        if more:
+            mixer_line = line_pieces(mixer_shards[i + 1], s)
+        signals = barrier(signal, partner, far, beyond)
+        gated, conv = conv_forward(place, *signals, windows[i], dft, inverse, gate, shift_all[i])
+        if more:
+            gated, feed_all_twin, mixer_line = barrier(gated, feed_all_twin, mixer_line)
+            feed_pieces[i] = [feed_shards[i], feed_all, twins[0], feed_all_twin]
+            mixer_line = jnp.stack(mixer_line)
+            mixer_plane = to_planes(mixer_line)
+            feed_line = line_pieces(feed_shards[i + 1], s)
+        else:
+            gated, feed_all_twin = barrier(gated, feed_all_twin)
+            feed_pieces[i] = [feed_shards[i], feed_all, twins[0], feed_all_twin]
+        before = stream
+        stream, middle, normed_mid, hidden, slope = feed_forward(
+            place, stream, gated, gain_all[i, 1:], bias_all[i, 1:], mixer_pieces[i], feed_pieces[i]
+        )
+        kept.append((before, normed_in, projected, edge, signals, gate, gated, conv, middle, normed_mid, hidden, slope))
+        if more:
+            stream, mixer_line, mixer_plane, feed_line = barrier(stream, mixer_line, mixer_plane, feed_line)
+            above = chan_permute(stream[-EDGE:], ahead_one)
+            feed_all = share_planes(jnp.stack(feed_line))
+            mixer_all = in_order([mixer_line, *mixer_plane], s)
+            mixer_all_twin = across_cores(mixer_all)
+            mixer_all, mixer_all_twin, above = barrier(mixer_all, mixer_all_twin, above)
+            mixer_pieces[i + 1] = [mixer_shards[i + 1], mixer_all, twins[1], mixer_all_twin]
+            twins[0] = across_cores(feed_shards[i + 1])
+
+    def flat(part):
+        return part.reshape(4, 4, -1, width)
+
+    def small_sums(i, grads):
+        grad_last, g_middle, g_taps, g_shift = grads
+        first_sin = acts[i][1]
+        first_cos, middle_cos = cosines[i] or (jnp.cos(acts[i][0]), jnp.cos(acts[i][2]))
+        g_middle = g_middle * middle_cos
+        grad_middle = lax.dot_general(
+            first_sin, g_middle, (((0,), (0,)), ((), ())), precision=HIGHEST, preferred_element_type=F32
+        )
+        g_first = lax.dot_general(
+            g_middle, filter_mid[i], (((1,), (1,)), ((), ())), precision=HIGHEST, preferred_element_type=F32
+        ) * first_cos
+        grad_first = lax.dot_general(
+            features, g_first, (((0,), (0,)), ((), ())), precision=HIGHEST, preferred_element_type=F32
+        )
+        rest = jnp.concatenate([grad_first, grad_middle], axis=0).reshape(-1)
+        rest = jnp.pad(rest, (0, -rest.size % width)).reshape(-1, width)
+        return jnp.concatenate(
+            [grad_last, jnp.sum(g_taps, axis=1), jnp.sum(g_shift, axis=0)[None], rest], axis=0
+        )
+
+    def norm_sums(*grads):
+        return jnp.sum(jnp.stack(grads), axis=1)
+
+    def backward_feed(i, g_stream):
+        (_, _, _, _, _, gate, _, _, middle, _, _, slope) = kept[i]
+        return feed_backward(
+            place, g_stream, middle, gain_all[i, 1:], gate, slope, mixer_pieces[i], feed_pieces[i]
+        )
+
+    def backward_conv(i, g_gated, g_convs):
+        (_, _, projected, edge, signals, _, _, conv, _, _, _, _) = kept[i]
+        return conv_backward(
+            place, signals, g_convs, windows[i], dft, inverse, projected, edge, taps_all[i], shift_all[i], g_gated,
+            conv, rates, acts[i][4], last_all[i],
+        )
+
+    def mend(i, g_proj, g_ahead):
+        g_ahead = jnp.where(later > 0, g_ahead, 0).astype(F32)
+        taps_of = taps_all[i].reshape(3, 3, width)
+        last_fix = taps_of[1] * g_ahead[:, 0] + taps_of[2] * g_ahead[:, 1]
+        before_fix = taps_of[2] * g_ahead[:, 0]
+        fix = jnp.concatenate(
+            [jnp.zeros((3, EDGE - 2, width), F32), before_fix[:, None], last_fix[:, None]], axis=1
+        )
+        tail = (g_proj[:, -EDGE:].astype(F32) + fix).astype(BF16)
+        return lax.dynamic_update_slice(g_proj, tail, (0, local_rows - EDGE, 0))
+
+    def out_grads(i, g_out):
+        return [flat(part) for part in grad_rows(place, kept[i][6], g_out[None])]
+
+    g_down, g_pre, g_mid, g_out, g_gated, g_conv, g_gain_two, g_bias_two = barrier(*backward_feed(1, cotangent))
+    partner = across_cores(g_conv)
+    far = chan_permute(g_conv, back)
+    down = grad_down(place, kept[1][10], g_down)
+    up = grad_up(place, kept[1][9], g_pre)
+    partner, far, down, up = barrier(partner, far, down, up)
+    beyond = across_cores(far)
+    out = out_grads(1, g_out)
+    beyond, out = barrier(beyond, out)
+    got = [across_cores(values[1]) for values in (up, down, out)]
+    g_proj, g_edge, *filter_grads = backward_conv(1, g_gated, (g_conv, partner, far, beyond))
+    g_proj, g_edge, got, filter_grads = barrier(g_proj, g_edge, got, filter_grads)
+    g_ahead = chan_permute(g_edge, back_one)
+    feed_one = merge_cores(place, (up[0], down[0]), got[:2], "whole")[0]
+    g_ahead, feed_one = barrier(g_ahead, feed_one)
+    feed_one = scatter_planes(feed_one)
+    g_proj = mend(1, g_proj, g_ahead)
+    in_one = [flat(part) for part in grad_rows(place, kept[1][1], g_proj)]
+    in_one, g_proj = barrier(in_one, g_proj)
+    in_got = across_cores(in_one[1])
+    g_stream, g_gain_one, g_bias_one = project_backward(
+        place, g_proj, kept[1][0], g_mid, gain_all[1, :1], mixer_pieces[1]
+    )
+    g_stream, in_got, g_gain_one, g_bias_one = barrier(g_stream, in_got, g_gain_one, g_bias_one)
+    norms_one = norm_sums(g_gain_one, g_gain_two, g_bias_one, g_bias_two)
+    results, feed_one = barrier(backward_feed(0, g_stream), feed_one)
+    ones = merge_cores(place, (out[0], in_one[0]), (got[2], in_got), "whole")[0]
+    ones, results = barrier(ones, results)
+    ones = scatter_planes(ones)
+    g_down, g_pre, g_mid, g_out, g_gated, g_conv, g_gain_two, g_bias_two = results
+    partner = across_cores(g_conv)
+    far = chan_permute(g_conv, back)
+    down = grad_down(place, kept[0][10], g_down)
+    small_one = jnp.concatenate([small_sums(1, filter_grads), norms_one])
+    partner, far, down, small_one = barrier(partner, far, down, small_one)
+    beyond = across_cores(far)
+    down_got = across_cores(down[1])
+    small_got = across_cores(small_one)
+    up = grad_up(place, kept[0][9], g_pre)
+    beyond, down_got, up, small_got, ones = barrier(beyond, down_got, up, small_got, ones)
+    up_got = across_cores(up[1])
+    small_one = small_one + small_got
+    small_got = across_line(small_one, 1)
+    out = out_grads(0, g_out)
+    up_got, out, small_got = barrier(up_got, out, small_got)
+    out_got = across_cores(out[1])
+    small_one = small_one + small_got
+    feed_zero = merge_cores(place, (up[0], down[0], out[0]), (up_got, down_got, out_got), "halves")
+    feed_zero, small_one, ones = barrier(feed_zero, small_one, ones)
+    ones = scatter_lines(jnp.concatenate([feed_one, ones], axis=1))
+    feed_got = [across_plane(feed_zero[1], 1), across_plane(feed_zero[3], 2)]
+    small_got = across_line(small_one, 2)
+    g_proj, g_edge, *filter_grads = backward_conv(0, g_gated, (g_conv, partner, far, beyond))
+    g_proj, g_edge, filter_grads, small_got, ones, feed_got = barrier(
+        g_proj, g_edge, filter_grads, small_got, ones, feed_got
+    )
+    ones = share_planes(ones)
+    feed_sent = [add_all(feed_zero[2 * side][1], [feed_got[side][1]]) for side in range(2)]
+    last_got = [across_plane(feed_sent[0], 2), across_plane(feed_sent[1], 1)]
+    g_ahead = chan_permute(g_edge, back_one)
+    small_one = small_one + small_got
+    g_ahead, small_one = barrier(g_ahead, small_one)
+    small_got = across_plane(small_one, 1)
+    g_proj = mend(0, g_proj, g_ahead)
+    in_zero = [flat(part) for part in grad_rows(place, kept[0][1], g_proj)]
+    in_zero, g_proj, small_got, last_got = barrier(in_zero, g_proj, small_got, last_got)
+    in_got = across_cores(in_zero[1])
+    small_one = small_one + small_got
+    small_zero = small_sums(0, filter_grads)
+    small_zero, in_got, small_one, g_proj = barrier(small_zero, in_got, small_one, g_proj)
+    feed_zero = jnp.concatenate(
+        [add_all(feed_zero[2 * side][0], [feed_got[side][0], last_got[side]]) for side in range(2)], axis=1
+    )
+    feed_got = send_lines(feed_zero, z, (1,))
+    in_zero = merge_cores(place, in_zero[:1], [in_got], "hops")
+    in_zero, feed_zero, g_proj, feed_got = barrier(in_zero, feed_zero, g_proj, feed_got)
+    in_got = send_planes(in_zero)
+    feed_got = feed_got + send_lines(feed_zero, z, (2,))
+    small_got = across_cores(small_zero)
+    g_stream, g_gain_one, g_bias_one = project_backward(
+        place, g_proj, kept[0][0], g_mid, gain_all[0, :1], mixer_pieces[0]
+    )
+    g_stream, g_gain_one, g_bias_one, in_got, feed_got, small_got = barrier(
+        g_stream, g_gain_one, g_bias_one, in_got, feed_got, small_got
+    )
+    in_zero = add_all(in_zero[0], in_got)
+    in_got = send_lines(in_zero, z)
+    feed_got = feed_got + send_lines(feed_zero, z, (3,))
+    norms = norm_sums(g_gain_one, g_gain_two, g_bias_one, g_bias_two)
+    norms = norms + across_cores(norms)
+    small_zero = jnp.concatenate([small_zero + small_got, norms])
+    feed_got, in_got, small_zero = barrier(feed_got, in_got, small_zero)
+    feed_zero = add_all(pick(feed_zero, z), feed_got)
+    in_zero = add_all(pick(in_zero, z), in_got)
+    zeros = jnp.concatenate([feed_zero, in_zero])
+    zeros_got = to_planes(zeros)
+    small_one = small_one + across_plane(small_one, 2)
+    small_zero = small_zero + across_line(small_zero, 1)
+    small_zero = small_zero + across_line(small_zero, 2)
+    small_zero = small_zero + across_plane(small_zero, 1)
+    small_zero, zeros_got, small_one = barrier(small_zero, zeros_got, small_one)
+    small_got = across_plane(small_zero, 2)
+    grad_up_all, grad_down_all, grad_out_all, grad_in_all = lay_out(place, ones, [zeros, *zeros_got])
+    grad_up_all, small_got = barrier(grad_up_all, small_got)
+    wide = jnp.stack([small_zero + small_got, small_one])
+    mine = lax.dynamic_slice_in_dim(wide, chan_index * chan_width, chan_width, axis=2)
+    rest = wide[:, hid + 10 : -4].reshape(LAYERS, -1)
+    first_size = filter_first.shape[1] * hid
+    return (
+        stream,
+        g_stream,
+        mine[:, -4:-2],
+        mine[:, -2:],
+        grad_in_all,
+        mine[:, hid : hid + 9].reshape(LAYERS, 3, 3, chan_width),
+        rest[:, :first_size].reshape(filter_first.shape),
+        rest[:, first_size : first_size + hid * hid].reshape(filter_mid.shape),
+        mine[:, :hid],
+        mine[:, hid + 9],
+        grad_out_all,
+        grad_up_all,
+        grad_down_all,
+    )
+
+
+def fits_sequence_form(mesh):
+    return mesh.shape["chan"] == 8 and mesh.shape["seq"] == 4
+
+
 def solution(mesh):
+    body, chan = local, "chan"
+    if fits_sequence_form(mesh):
+        body, chan = sequence_local, ("line", "core")
+        mesh = Mesh(mesh.devices.reshape(4, 4, 2), ("seq", "line", "core"))
+    rows = ("seq", *chan) if body is sequence_local else ("seq", chan)
     in_specs = (
-        P(("seq", "chan"), None),
-        P(None, None, "chan"),
-        P(None, None, "chan"),
-        P(None, "chan", None),
-        P(None, None, None, "chan"),
+        P(rows, None),
+        P(None, None, chan),
+        P(None, None, chan),
+        P(None, chan, None),
+        P(None, None, None, chan),
         P(),
         P(),
-        P(None, None, "chan"),
-        P(None, "chan"),
-        P(None, "chan", None),
-        P(None, "chan", None),
-        P(None, "chan", None),
+        P(None, None, chan),
+        P(None, chan),
+        P(None, chan, None),
+        P(None, chan, None),
+        P(None, chan, None),
         P(),
         P(),
         P(),
-        P(("seq", "chan"), None),
+        P(rows, None),
     )
     out_specs = (
-        P(("seq", "chan"), None),
-        P(("seq", "chan"), None),
-        P(None, None, "chan"),
-        P(None, None, "chan"),
-        P(None, "chan", None),
-        P(None, None, None, "chan"),
+        P(rows, None),
+        P(rows, None),
+        P(None, None, chan),
+        P(None, None, chan),
+        P(None, chan, None),
+        P(None, None, None, chan),
         P(),
         P(),
-        P(None, None, "chan"),
-        P(None, "chan"),
-        P(None, "chan", None),
-        P(None, "chan", None),
-        P(None, "chan", None),
-    )
-    return jax.shard_map(local, mesh=mesh, in_specs=in_specs, out_specs=out_specs, check_vma=False)
+        P(None, None, chan),
+        P(None, chan),
+        P(None, chan, None),
+        P(None, chan, None),
+        P(None, chan, None),
+    )
+    return jax.shard_map(body, mesh=mesh, in_specs=in_specs, out_specs=out_specs, check_vma=False)

time: 4970 us -> 1150 us (0.23)
  matrix products: 1530 us -> 59.6 us
  local copies, waits for them, and re-layouts: 1150 us -> 134 us
  waiting for transfers between devices: 1020 us -> 208 us
  other arithmetic: 753 us -> 65 us
  Pallas kernels: 0 us -> 533 us
  blocking collectives: 382 us -> 0 us
  starting transfers between devices: 35.7 us -> 126 us
  loops' own time: 57.2 us -> 0 us
    dot_general x102 -> x6, matrix products: 1520 us -> 36.9 us  [the longest x2 19.9 us: small_sums(): lax.dot_general(g_middle, filter_mid[i], (((1,), (1,)), ((), ())), precis...]
    all_to_all x7 -> x0, waiting for transfers between devices: 810 us -> none  [the longest x2 389 us: local(): lax.all_to_all(proj_cols, 'chan', split_axis=1, concat_axis=2, tiled=True)]
    pallas_call x0 -> x28, Pallas kernels: none -> 533 us  [the longest x2 109 us: conv_backward(): pl.pallas_call(conv_backward_kernel, grid_spec=pltpu.PrefetchScalarGridSp...]
    reduce_sum x22 -> x6, other arithmetic: 258 us -> 1.24 us  [the longest x2 1.11 us: small_sums(): jnp.sum(g_taps, axis=1)]
    all_to_all x1 -> x0, blocking collectives: 195 us -> none  [local(): lax.all_to_all(grad_proj.astype(jnp.bfloat16), 'chan', split_axis=2, conc...]
    ppermute x0 -> x83, waiting for transfers between devices: none -> 191 us  [the longest x24 90.6 us: across_line(): return lax.ppermute(values, 'line', xor_pairs(lax.axis_size('line'), hop))]
    another operation x46 -> x7, local copies, waits for them, and re-layouts: 185 us -> 5.42 us  [the longest x2 2.86 us: feed_shard(): up = up_weight[layer_index].reshape(chan_width, 4, width).transpose(1, 0, 2)]
    reshape x14 -> x8, local copies, waits for them, and re-layouts: 147 us -> 2.99 us  [the longest x1 1.99 us: sequence_local(): small = in_channel_order(place, small).reshape(LAYERS, hid + 14, width)]
  transfers between devices with their start and end apart: 32 -> 88, of which waited for: 13 -> 26; matrix products, arithmetic and copies ran while one was open for 52% -> 14% of each run, Pallas kernels for 0% -> 39%
where the time goes in v1:
time: 1150 us; the launch traced here: 1140 us
  Pallas kernels  533 us (46%)
  waiting for transfers between devices  208 us (18%)
  local copies, waits for them, and re-layouts  134 us (12%)
  starting transfers between devices  126 us (11%)
  other arithmetic  65 us (6%)
  matrix products  59.6 us (5%)
  between operations  16.9 us (1%)
    pallas_call x2, Pallas kernels, conv_backward(): pl.pallas_call(conv_backward_kernel, grid_spec=pltpu.PrefetchScalarGridSp...  109 us
    ppermute x24, waiting for transfers between devices, across_line(): return lax.ppermute(values, 'line', xor_pairs(lax.axis_size('line'), hop))  90.6 us
    pallas_call x2, Pallas kernels, feed_forward(): pl.pallas_call(feed_kernel, grid_spec=pltpu.PrefetchScalarGridSpec(num_sc...  86.8 us
    pallas_call x2, Pallas kernels, feed_backward(): pl.pallas_call(feed_backward_kernel, grid_spec=pltpu.PrefetchScalarGridSp...  79.2 us
    unnamed x324, local copies, waits for them, and re-layouts  74.2 us
    ppermute x24, starting transfers between devices, across_line(): return lax.ppermute(values, 'line', xor_pairs(lax.axis_size('line'), hop))  53.1 us
    ppermute x23, waiting for transfers between devices, across_plane(): return lax.ppermute(values, 'seq', xor_pairs(lax.axis_size('seq'), hop))  43.7 us
    pallas_call x2, Pallas kernels, window_spectra(): pl.pallas_call(window_kernel, grid_spec=pltpu.PrefetchScalarGridSpec(num_...  41.2 us
  transfers between devices with their start and end apart: 88, of which 26 were waited for; matrix products, arithmetic and copies ran while one was open for 14% of the time, Pallas kernels for 39%

profile of v1, /device:TPU:0, one launch (start us, length us, event | category | flops | bytes accessed | tf_op | source)
XLA Modules:
  0.0 1143.5 jit_solution(16670757878177234383)
XLA Ops:
  34.3 13.8 %collective-permute-done.8 = f32[2,156,128]{2,1,0:T(8,128)S(1)} collective-permute-done((f32[2,156,128]{2,1,0:T(8,128)S(1)}, f32[2,156,128]{2,1,0:T(8,128)S(1)}, u32[]{:S(2)}, u32[]{:S(2)}) %collective-permute-start.8) | collective-permute-done | bytes 159776 | tf_op jit(solution)/shard_map/ppermute | solution.py:1502
  50.2 5.7 fusion.96
  55.9 5.7 fusion.94
  66.7 5.7 fusion.97
  72.6 5.7 fusion.95
  84.1 20.5 %collective-permute-done.10 = bf16[2,128,1024]{2,1,0:T(8,128)(2,1)S(1)} collective-permute-done((bf16[2,128,1024]{2,1,0:T(8,128)(2,1)}, bf16[2,128,1024]{2,1,0:T(8,128)(2,1)S(1)}, u32[]{:S(2)}, u32[]{:S(2)}) %collective-permute-start.10) | collective-permute-done | bytes 524320 | tf_op jit(solution)/shard_map/ppermute | solution.py:1502
  111.5 13.3 %collective-permute-start.13 = (f32[16,1024]{1,0:T(8,128)S(1)}, f32[16,1024]{1,0:T(8,128)S(1)}, u32[]{:S(2)}, u32[]{:S(2)}) collective-permute-start(f32[16,1024]{1,0:T(8,128)S(1)} %slice.217), channel_id=1, source_target_pairs={{0,1},{1,2},{2,3},{4,5},{5,6},{6,7},{8,9},{9,10},{10,11},{12,13},{... | collective-permute-start | bytes 196616 | tf_op jit(solution)/shard_map/ppermute | solution.py:1578
  124.8 5.7 in_channel_order.1
  142.7 19.0 %project.2 = (bf16[1024,1024]{1,0:T(8,128)(2,1)S(1)}, bf16[1024,1024]{1,0:T(8,128)(2,1)}, bf16[1024,1024]{1,0:T(8,128)(2,1)}, bf16[1024,1024]{1,0:T(8,128)(2,1)}...) custom-call(s32[8]{0:T(128)S(1)} %copy-done.62, f32[1024,1024]{1,0:T(8,128)} %stream.5, ...), custom_call_target="tpu_custom_call" | custom-call | flops 1000 | bytes 1000 | tf_op jit(solution)/shard_map/project/pallas_call | solution.py:991
  163.6 8.2 collective-permute-done.15
  185.3 20.5 %window_spectra.2.window_ref = bf16[8,1024,1024]{2,1,0:T(8,128)(2,1)S(1)} custom-call(s32[8]{0:T(128)S(1)} %copy-done.62, bf16[4096,192]{1,0:T(8,128)(2,1)S(1)} %copy-done.17, bf16[192,1024]{1,0:T(8,128)(2,1)S(1)} %pad_maximum_fusion.21.last_ref, f32[1,1024]{1,0:T(1,128)S(1)} %add_exponential_fusion.rate_ref, bf16[2,512,256]{2,1,0:T(8,128)(2,1)S(1)} %copy-done.10), custom_call_target="tpu_custom_call" | custom-call | flops 1000 | bytes 1000 | tf_op jit(solution)/shard_map/window_spectra/pallas_call | solution.py:484
  205.9 5.7 copy-done
  243.5 12.3 %conv_forward.2 = (bf16[1024,1024]{1,0:T(8,128)(2,1)S(1)}, bf16[1024,1024]{1,0:T(8,128)(2,1)S(1)}) custom-call(s32[8]{0:T(128)S(1)} %copy-done.62, bf16[1024,1024]{1,0:T(8,128)(2,1)} %get-tuple-element.337.own, bf16[1024,1024]{1,0:T(8,128)(2,1)} %collective-permute-done.20.partner, bf16[1024,1024]{1,0:T(8,128)(2,1)} %collective-permute-done.19.far, ...), custom_call_target="tpu_custom_call" | custom-call | flops 1000 | bytes 1000 | tf_op jit(solution)/shard_map/conv_forward/pallas_call | solution.py:611
  266.7 7.4 collective-permute-start.32
  274.1 43.6 %feed_forward.2 = (f32[1024,1024]{1,0:T(8,128)}, f32[1024,1024]{1,0:T(8,128)}, bf16[1024,1024]{1,0:T(8,128)(2,1)}, bf16[1024,4096]{1,0:T(8,128)(2,1)}, bf16[1024,4096]{1,0:T(8,128)(2,1)}) custom-call(s32[8]{0:T(128)} %stack.200.place_ref, f32[1024,1024]{1,0:T(8,128)} %stream.5, bf16[1024,1024]{1,0:T(8,128)(2,1)} %copy-done.18, ...), custom_call_target="tpu_custom_call" | custom-call | flops 1000 | bytes 1000 | tf_op jit(solution)/shard_map/feed_forward/pallas_call | solution.py:1088
  334.3 18.8 %project.3 = (bf16[1024,1024]{1,0:T(8,128)(2,1)S(1)}, bf16[1024,1024]{1,0:T(8,128)(2,1)}, bf16[1024,1024]{1,0:T(8,128)(2,1)}, bf16[1024,1024]{1,0:T(8,128)(2,1)}...) custom-call(s32[8]{0:T(128)S(1)} %copy-done.63, ...), custom_call_target="tpu_custom_call" | custom-call | flops 1000 | bytes 1000 | tf_op jit(solution)/shard_map/project/pallas_call | solution.py:991
  365.9 9.6 cos.17
  379.8 20.7 %window_spectra.3.window_ref = bf16[8,1024,1024]{2,1,0:T(8,128)(2,1)S(1)} custom-call(s32[8]{0:T(128)S(1)} %copy-done.63, bf16[4096,192]{1,0:T(8,128)(2,1)S(1)} %copy-done.16, bf16[192,1024]{1,0:T(8,128)(2,1)S(1)} %pad_maximum_fusion.22.last_ref, f32[1,1024]{1,0:T(1,128)S(1)} %add_exponential_fusion.rate_ref, bf16[2,512,256]{2,1,0:T(8,128)(2,1)S(1)} %copy-done.11), custom_call_target="tpu_custom_call" | custom-call | flops 1000 | bytes 1000 | tf_op jit(solution)/shard_map/window_spectra/pallas_call | solution.py:484
  400.5 5.9 copy-done.1
  408.5 10.0 collective-permute-done.37.beyond
  419.8 12.1 %conv_forward.3 = (bf16[1024,1024]{1,0:T(8,128)(2,1)S(1)}, bf16[1024,1024]{1,0:T(8,128)(2,1)S(1)}) custom-call(s32[8]{0:T(128)S(1)} %copy-done.63, bf16[1024,1024]{1,0:T(8,128)(2,1)} %get-tuple-element.376.own, bf16[1024,1024]{1,0:T(8,128)(2,1)} %collective-permute-done.36.partner, bf16[1024,1024]{1,0:T(8,128)(2,1)} %collective-permute-done.35.far, ...), custom_call_target="tpu_custom_call" | custom-call | flops 1000 | bytes 1000 | tf_op jit(solution)/shard_map/conv_forward/pallas_call | solution.py:611
  435.9 43.2 %feed_forward.3 = (f32[1024,1024]{1,0:T(8,128)}, f32[1024,1024]{1,0:T(8,128)}, bf16[1024,1024]{1,0:T(8,128)(2,1)}, bf16[1024,4096]{1,0:T(8,128)(2,1)}, bf16[1024,4096]{1,0:T(8,128)(2,1)}) custom-call(s32[8]{0:T(128)} %stack.200.place_ref, f32[1024,1024]{1,0:T(8,128)} %get-tuple-element.354.stream, bf16[1024,1024]{1,0:T(8,128)(2,1)} %copy-done.20, ...), custom_call_target="tpu_custom_call" | custom-call | flops 1000 | bytes 1000 | tf_op jit(solution)/shard_map/feed_forward/pallas_call | solution.py:1088
  479.1 39.3 %feed_backward.2 = (bf16[1024,1024]{1,0:T(8,128)(2,1)}, bf16[1024,4096]{1,0:T(8,128)(2,1)}, f32[1024,1024]{1,0:T(8,128)}, bf16[1024,1024]{1,0:T(8,128)(2,1)}, bf...) custom-call(s32[8]{0:T(128)} %stack.200.place_ref, ...), custom_call_target="tpu_custom_call" | custom-call | flops 1000 | bytes 1000 | tf_op jit(solution)/shard_map/feed_backward/pallas_call | solution.py:1202
  523.3 13.5 %grad_up.2 = (bf16[4,4,128,1024]{3,2,1,0:T(8,128)(2,1)S(1)}, bf16[4,4,128,1024]{3,2,1,0:T(8,128)(2,1)}) custom-call(s32[8]{0:T(128)S(1)} %copy-done.64, bf16[1024,1024]{1,0:T(8,128)(2,1)S(1)} %copy-done.50, bf16[1024,4096]{1,0:T(8,128)(2,1)} %get-tuple-element.396.g_pre), custom_call_target="tpu_custom_call" | custom-call | flops 1000 | bytes 1000 | tf_op jit(solution)/shard_map/grad_up/pallas_call | solution.py:1304
  538.8 14.0 %grad_down.2 = (bf16[4,4,128,1024]{3,2,1,0:T(8,128)(2,1)S(1)}, bf16[4,4,128,1024]{3,2,1,0:T(8,128)(2,1)}) custom-call(s32[8]{0:T(128)S(1)} %copy-done.64, bf16[1024,4096]{1,0:T(8,128)(2,1)} %get-tuple-element.391.hidden, bf16[1024,1024]{1,0:T(8,128)(2,1)S(1)} %copy-done.51), custom_call_target="tpu_custom_call" | custom-call | flops 1000 | bytes 1000 | tf_op jit(solution)/shard_map/grad_down/pallas_call | solution.py:1332
  554.8 23.4 %collective-permute-done.41.g_far = bf16[1024,1024]{1,0:T(8,128)(2,1)S(1)} collective-permute-done((bf16[1024,1024]{1,0:T(8,128)(2,1)}, bf16[1024,1024]{1,0:T(8,128)(2,1)S(1)}, u32[]{:S(2)}, u32[]{:S(2)}) %collective-permute-start.41) | collective-permute-done | bytes 2097184 | tf_op jit(solution)/shard_map/ppermute | solution.py:1578
  582.9 7.6 collective-permute-done.42.g_beyond
  592.0 54.3 %conv_backward.2 = (bf16[3,1024,1024]{2,1,0:T(8,128)(2,1)}, bf16[3,16,1024]{2,1,0:T(8,128)(2,1)}, f32[64,1024]{1,0:T(8,128)}, f32[4096,64]{1,0:T(8,128)}, f32[9,8,1024]{2,1,0:T(8,128)}, /*index=5*/f32[8,1024]{1,0:T(8,128)}) custom-call(s32[8]{0:T(128)} %stack.200.place_ref, bf16[1024,1024]{1,0:T(8,128)(2,1)} %get-tuple-element.376.own, ...), custom_call_target="tpu_custom_call" | custom-call | flops 1000 | bytes 1000 | tf_op jit(solution)/shard_map/conv_backward/pallas_call | solution.py:806
  652.9 8.5 merge_cores.4
  665.1 11.4 grad_rows.5
  681.8 19.8 %project_backward.2 = (f32[1024,1024]{1,0:T(8,128)}, f32[8,1024]{1,0:T(8,128)S(1)}, f32[8,1024]{1,0:T(8,128)S(1)}) custom-call(s32[8]{0:T(128)S(1)} %copy-done.65, bf16[3,1024,1024]{2,1,0:T(8,128)(2,1)} %fusion.33.right.g_proj, f32[1024,1024]{1,0:T(8,128)} %get-tuple-element.354.stream, f32[1024,1024]{1,0:T(8,128)} %get-tuple-element.435.g_mid, ...), custom_call_target="tpu_custom_call" | custom-call | flops 1000 | bytes 1000 | tf_op jit(solution)/shard_map/project_backward/pallas_call | solution.py:1264
  703.2 39.9 %feed_backward.3 = (bf16[1024,1024]{1,0:T(8,128)(2,1)}, bf16[1024,4096]{1,0:T(8,128)(2,1)}, f32[1024,1024]{1,0:T(8,128)}, bf16[1024,1024]{1,0:T(8,128)(2,1)}, bf...) custom-call(s32[8]{0:T(128)} %stack.200.place_ref, ...), custom_call_target="tpu_custom_call" | custom-call | flops 1000 | bytes 1000 | tf_op jit(solution)/shard_map/feed_backward/pallas_call | solution.py:1202
  749.7 8.5 reduce-scatter.10.cloned.1.call-done
  761.6 14.7 %convolution_multiply_fusion.1 = f32[4096,64]{0,1:T(8,128)S(1)} fusion(f32[4096,64]{0,1:T(8,128)} %get-tuple-element.471, f32[4096,64]{1,0:T(8,128)} %get-tuple-element.469, f32[4096,64]{1,0:T(8,128)S(1)} %copy.159, f32[2,64,64]{2,1,0:T(8,128)S(1)} %copy-done.139), kind=kOutput, calls=%fused_computation.3 | convolution fusion | flops 201850880 | bytes 5275648 | tf_op jit(solution)/shard_map/dot_general | solution.py:1772
  777.6 11.6 %fusion.10 = f32[64,64]{0,1:T(8,128)S(1)} fusion(f32[4096,64]{0,1:T(8,128)S(1)} %copy-done.87, f32[4096,64]{1,0:T(8,128)S(1)} %copy-done.90, f32[4096,64]{1,0:T(8,128)} %copy-done.79), kind=kOutput, calls=%fused_computation.47 | convolution fusion | flops 201588736 | bytes 3162112 | tf_op jit(solution)/shard_map/dot_general | solution.py:1769
  789.9 13.2 %grad_down.3 = (bf16[4,4,128,1024]{3,2,1,0:T(8,128)(2,1)S(1)}, bf16[4,4,128,1024]{3,2,1,0:T(8,128)(2,1)S(1)}) custom-call(s32[8]{0:T(128)S(1)} %copy-done.66, bf16[1024,4096]{1,0:T(8,128)(2,1)} %get-tuple-element.462.hidden, bf16[1024,1024]{1,0:T(8,128)(2,1)S(1)} %copy-done.49), custom_call_target="tpu_custom_call" | custom-call | flops 1000 | bytes 1000 | tf_op jit(solution)/shard_map/grad_down/pallas_call | solution.py:1332
  809.2 12.6 %grad_up.3 = (bf16[4,4,128,1024]{3,2,1,0:T(8,128)(2,1)S(1)}, bf16[4,4,128,1024]{3,2,1,0:T(8,128)(2,1)S(1)}) custom-call(s32[8]{0:T(128)S(1)} %copy-done.66, bf16[1024,1024]{1,0:T(8,128)(2,1)S(1)} %copy-done.46, bf16[1024,4096]{1,0:T(8,128)(2,1)} %get-tuple-element.481.g_pre), custom_call_target="tpu_custom_call" | custom-call | flops 1000 | bytes 1000 | tf_op jit(solution)/shard_map/grad_up/pallas_call | solution.py:1304
  839.5 7.8 merge_cores.6
  858.0 54.5 %conv_backward.3 = (bf16[3,1024,1024]{2,1,0:T(8,128)(2,1)}, bf16[3,16,1024]{2,1,0:T(8,128)(2,1)}, f32[64,1024]{1,0:T(8,128)}, f32[4096,64]{1,0:T(8,128)}, f32[9,8,1024]{2,1,0:T(8,128)}, /*index=5*/f32[8,1024]{1,0:T(8,128)}) custom-call(s32[8]{0:T(128)} %stack.200.place_ref, bf16[1024,1024]{1,0:T(8,128)(2,1)} %get-tuple-element.337.own, ...), custom_call_target="tpu_custom_call" | custom-call | flops 1000 | bytes 1000 | tf_op jit(solution)/shard_map/conv_backward/pallas_call | solution.py:806
  912.5 9.0 reduce-scatter.8.cloned.1.call-done
  934.4 11.1 grad_rows.7
  947.2 11.6 %collective-permute-done.60 = f32[85,1024]{1,0:T(8,128)S(1)} collective-permute-done((f32[85,1024]{1,0:T(8,128)S(1)}, f32[85,1024]{1,0:T(8,128)S(1)}, u32[]{:S(2)}, u32[]{:S(2)}) %collective-permute-start.60) | collective-permute-done | bytes 348192 | tf_op jit(solution)/shard_map/ppermute | solution.py:1506
  1003.3 19.8 %project_backward.3 = (f32[1024,1024]{1,0:T(8,128)}, f32[8,1024]{1,0:T(8,128)S(1)}, f32[8,1024]{1,0:T(8,128)S(1)}) custom-call(s32[8]{0:T(128)S(1)} %copy-done.67, bf16[3,1024,1024]{2,1,0:T(8,128)(2,1)} %fusion.32.right.g_proj, f32[1024,1024]{1,0:T(8,128)} %stream.5, f32[1024,1024]{1,0:T(8,128)} %get-tuple-element.553.g_mid, f32[1,1024]{1,0:T(1,128)S(1)} %copy-done.72, ...), custom_call_target="tpu_custom_call" | custom-call | flops 1000 | bytes 1000 | tf_op jit(solution)/shard_map/project_backward/pallas_call | solution.py:1264
  1024.8 18.3 %collective-permute-done.68 = bf16[288,1024]{1,0:T(8,128)(2,1)S(1)} collective-permute-done((bf16[288,1024]{1,0:T(8,128)(2,1)S(1)}, bf16[288,1024]{1,0:T(8,128)(2,1)S(1)}, u32[]{:S(2)}, u32[]{:S(2)}) %collective-permute-start.68) | collective-permute-done | bytes 589856 | tf_op jit(solution)/shard_map/ppermute | solution.py:1502
  1053.4 14.9 %collective-permute-done.72 = bf16[96,1024]{1,0:T(8,128)(2,1)S(1)} collective-permute-done((bf16[96,1024]{1,0:T(8,128)(2,1)}, bf16[96,1024]{1,0:T(8,128)(2,1)S(1)}, u32[]{:S(2)}, u32[]{:S(2)}) %collective-permute-start.72) | collective-permute-done | bytes 196640 | tf_op jit(solution)/shard_map/ppermute | solution.py:1502
  1085.7 14.6 %collective-permute-done.76 = f32[85,1024]{1,0:T(8,128)S(1)} collective-permute-done((f32[85,1024]{1,0:T(8,128)S(1)}, f32[85,1024]{1,0:T(8,128)S(1)}, u32[]{:S(2)}, u32[]{:S(2)}) %collective-permute-start.76) | collective-permute-done | bytes 348192 | tf_op jit(solution)/shard_map/ppermute | solution.py:1502
  1101.4 19.1 %collective-permute-done.81 = f32[85,1024]{1,0:T(8,128)S(1)} collective-permute-done((f32[85,1024]{1,0:T(8,128)S(1)}, f32[85,1024]{1,0:T(8,128)S(1)}, u32[]{:S(2)}, u32[]{:S(2)}) %collective-permute-start.81) | collective-permute-done | bytes 348192 | tf_op jit(solution)/shard_map/ppermute | solution.py:1506
  1125.3 6.0 lay_out.1
  (622 shorter events, 334.8 us)
Async XLA Ops:
  7.2 399.2 %all-gather.5.cloned.1.call-start = ((), (), s32[]{:S(2)}) async-start(), calls=%async_computation.4 | async-start | bytes 7864320 | tf_op jit(solution)/shard_map/all_gather | solution.py:1555
  11.7 38.5 %collective-permute-start = (bf16[1,128,1024]{2,1,0:T(8,128)(2,1)}, bf16[1,128,1024]{2,1,0:T(8,128)(2,1)}, u32[]{:S(2)}, u32[]{:S(2)}) collective-permute-start(bf16[1,128,1024]{2,1,0:T(8,128)(2,1)} %fusion.25), channel_id=1, source_target_pairs={{0,2},{2,0},{4,6},{6,4},{1,3},{3,1},{5,7},{7,5},{8,10},{10,8},{12,... | collective-permute-start | bytes 786440 | tf_op jit(solution)/shard_map/ppermute | solution.py:1502
  14.7 35.4 %collective-permute-start.1 = (bf16[1,128,1024]{2,1,0:T(8,128)(2,1)}, bf16[1,128,1024]{2,1,0:T(8,128)(2,1)}, u32[]{:S(2)}, u32[]{:S(2)}) collective-permute-start(bf16[1,128,1024]{2,1,0:T(8,128)(2,1)} %fusion.25), channel_id=1, source_target_pairs={{0,4},{2,6},{4,0},{6,2},{1,5},{3,7},{5,1},{7,3},{8,12},{10,14},{12... | collective-permute-start | bytes 786440 | tf_op jit(solution)/shard_map/ppermute | solution.py:1502
  17.3 32.9 %collective-permute-start.2 = (bf16[1,128,1024]{2,1,0:T(8,128)(2,1)}, bf16[1,128,1024]{2,1,0:T(8,128)(2,1)}, u32[]{:S(2)}, u32[]{:S(2)}) collective-permute-start(bf16[1,128,1024]{2,1,0:T(8,128)(2,1)} %fusion.25), channel_id=1, source_target_pairs={{0,6},{2,4},{4,2},{6,0},{1,7},{3,5},{5,3},{7,1},{8,14},{10,12},{12... | collective-permute-start | bytes 786440 | tf_op jit(solution)/shard_map/ppermute | solution.py:1502
  48.1 35.1 %collective-permute-start.9 = (f32[4,156,128]{2,1,0:T(8,128)S(1)}, f32[4,156,128]{2,1,0:T(8,128)S(1)}, u32[]{:S(2)}, u32[]{:S(2)}) collective-permute-start(f32[4,156,128]{2,1,0:T(8,128)S(1)} %pad_maximum_fusion.25), channel_id=1, source_target_pairs={{0,4},{2,6},{4,0},{6,2},{1,5},{3,7},{5,1},{7,3},{8,12},{10,14},{12... | collective-permute-start | bytes 958472 | tf_op jit(solution)/shard_map/ppermute | solution.py:1502
  63.2 41.4 %collective-permute-start.4 = (bf16[3,1,128,1024]{3,2,0,1:T(8,128)(2,1)S(1)}, bf16[3,1,128,1024]{3,2,0,1:T(8,128)(2,1)S(1)}, u32[]{:S(2)}, u32[]{:S(2)}) collective-permute-start(bf16[3,1,128,1024]{3,2,0,1:T(8,128)(2,1)S(1)} %pad_maximum_fusion.16), channel_id=1, source_target_pairs={{0,8},{8,0},{16,24},{24,16},{1,9},{9,1},{17,25},{25,17},{2,10},{10... | collective-permute-start | bytes 2359304 | tf_op jit(solution)/shard_map/ppermute | solution.py:1506
  64.8 39.8 %collective-permute-start.5 = (bf16[3,1,128,1024]{3,2,0,1:T(8,128)(2,1)S(1)}, bf16[3,1,128,1024]{3,2,0,1:T(8,128)(2,1)S(1)}, u32[]{:S(2)}, u32[]{:S(2)}) collective-permute-start(bf16[3,1,128,1024]{3,2,0,1:T(8,128)(2,1)S(1)} %pad_maximum_fusion.16), channel_id=1, source_target_pairs={{0,16},{8,24},{16,0},{24,8},{1,17},{9,25},{17,1},{25,9},{2,18},{10... | collective-permute-start | bytes 2359304 | tf_op jit(solution)/shard_map/ppermute | solution.py:1506
  66.3 38.3 %collective-permute-start.6 = (bf16[3,1,128,1024]{3,2,0,1:T(8,128)(2,1)S(1)}, bf16[3,1,128,1024]{3,2,0,1:T(8,128)(2,1)S(1)}, u32[]{:S(2)}, u32[]{:S(2)}) collective-permute-start(bf16[3,1,128,1024]{3,2,0,1:T(8,128)(2,1)S(1)} %pad_maximum_fusion.16), channel_id=1, source_target_pairs={{0,24},{8,16},{16,8},{24,0},{1,25},{9,17},{17,9},{25,1},{2,26},{10... | collective-permute-start | bytes 2359304 | tf_op jit(solution)/shard_map/ppermute | solution.py:1506
  110.4 53.2 %collective-permute-start.17 = (bf16[4,2,128,1024]{3,2,1,0:T(8,128)(2,1)}, bf16[4,2,128,1024]{3,2,1,0:T(8,128)(2,1)}, u32[]{:S(2)}, u32[]{:S(2)}) collective-permute-start(bf16[4,2,128,1024]{3,2,1,0:T(8,128)(2,1)} %pad_maximum_fusion.8.rest_4_), channel_id=1, source_target_pairs={{0,1},{1,0},{2,3},{3,2},{4,5},{5,4},{6,7},{7,6},{8,9},{9,8},{10,11... | collective-permute-start | bytes 6291464 | tf_op jit(solution)/shard_map/ppermute | solution.py:1498
  135.2 36.6 %collective-permute-start.15 = (bf16[3,2,128,1024]{3,2,1,0:T(8,128)(2,1)}, bf16[3,2,128,1024]{3,2,1,0:T(8,128)(2,1)}, u32[]{:S(2)}, u32[]{:S(2)}) collective-permute-start(bf16[3,2,128,1024]{3,2,1,0:T(8,128)(2,1)} %pad_maximum_fusion.12), channel_id=1, source_target_pairs={{0,8},{8,0},{16,24},{24,16},{1,9},{9,1},{17,25},{25,17},{2,10},{10... | collective-permute-start | bytes 4718600 | tf_op jit(solution)/shard_map/ppermute | solution.py:1506
  136.6 36.3 %collective-permute-start.16 = (bf16[3,2,128,1024]{3,2,1,0:T(8,128)(2,1)}, bf16[3,2,128,1024]{3,2,1,0:T(8,128)(2,1)}, u32[]{:S(2)}, u32[]{:S(2)}) collective-permute-start(bf16[3,2,128,1024]{3,2,1,0:T(8,128)(2,1)} %pad_maximum_fusion.12), channel_id=1, source_target_pairs={{0,16},{8,24},{16,0},{24,8},{1,17},{9,25},{17,1},{25,9},{2,18},{10... | collective-permute-start | bytes 4718600 | tf_op jit(solution)/shard_map/ppermute | solution.py:1506
  172.9 46.6 %collective-permute-start.19 = (bf16[1024,1024]{1,0:T(8,128)(2,1)}, bf16[1024,1024]{1,0:T(8,128)(2,1)}, u32[]{:S(2)}, u32[]{:S(2)}) collective-permute-start(bf16[1024,1024]{1,0:T(8,128)(2,1)} %get-tuple-element.337.own), channel_id=1, source_target_pairs={{0,2},{1,3},{4,6},{5,7},{8,10},{9,11},{12,14},{13,15},{16,18},{17,... | collective-permute-start | bytes 6291464 | tf_op jit(solution)/shard_map/ppermute | solution.py:1578
  177.0 42.6 %collective-permute-start.20 = (bf16[1024,1024]{1,0:T(8,128)(2,1)}, bf16[1024,1024]{1,0:T(8,128)(2,1)}, u32[]{:S(2)}, u32[]{:S(2)}) collective-permute-start(bf16[1024,1024]{1,0:T(8,128)(2,1)} %get-tuple-element.337.own), channel_id=1, source_target_pairs={{0,1},{1,0},{2,3},{3,2},{4,5},{5,4},{6,7},{7,6},{8,9},{9,8},{10,11... | collective-permute-start | bytes 6291464 | tf_op jit(solution)/shard_map/ppermute | solution.py:1498
  177.0 38.0 %collective-permute-start.21 = (bf16[3,2,128,1024]{3,2,1,0:T(8,128)(2,1)}, bf16[3,2,128,1024]{3,2,1,0:T(8,128)(2,1)}, u32[]{:S(2)}, u32[]{:S(2)}) collective-permute-start(bf16[3,2,128,1024]{3,2,1,0:T(8,128)(2,1)} %pad_maximum_fusion.12), channel_id=1, source_target_pairs={{0,24},{8,16},{16,8},{24,0},{1,25},{9,17},{17,9},{25,1},{2,26},{10... | collective-permute-start | bytes 4718600 | tf_op jit(solution)/shard_map/ppermute | solution.py:1506
  227.5 31.0 %collective-permute-start.23 = (bf16[4,3,2,128,1024]{4,3,2,1,0:T(8,128)(2,1)}, bf16[4,3,2,128,1024]{4,3,2,1,0:T(8,128)(2,1)}, u32[]{:S(2)}, u32[]{:S(2)}) collective-permute-start(bf16[4,3,2,128,1024]{4,3,2,1,0:T(8,128)(2,1)} %pad_maximum_fusion.1.rest_5_), channel_id=1, source_target_pairs={{0,1},{1,0},{2,3},{3,2},{4,5},{5,4},{6,7},{7,6},{8,9},{9,8},{10,11... | collective-permute-start | bytes 18874376 | tf_op jit(solution)/shard_map/ppermute | solution.py:1498
  228.1 30.3 %collective-permute-start.24 = (bf16[1,128,1024]{2,1,0:T(8,128)(2,1)S(1)}, bf16[1,128,1024]{2,1,0:T(8,128)(2,1)S(1)}, u32[]{:S(2)}, u32[]{:S(2)}) collective-permute-start(bf16[1,128,1024]{2,1,0:T(8,128)(2,1)S(1)} %fusion.24), channel_id=1, source_target_pairs={{0,2},{2,0},{4,6},{6,4},{1,3},{3,1},{5,7},{7,5},{8,10},{10,8},{12,... | collective-permute-start | bytes 786440 | tf_op jit(solution)/shard_map/ppermute | solution.py:1502
  260.4 57.3 %collective-permute-start.27 = (bf16[3,1,128,1024]{3,2,0,1:T(8,128)(2,1)S(1)}, bf16[3,1,128,1024]{3,2,0,1:T(8,128)(2,1)S(1)}, u32[]{:S(2)}, u32[]{:S(2)}) collective-permute-start(bf16[3,1,128,1024]{3,2,0,1:T(8,128)(2,1)S(1)} %pad_maximum_fusion.17), channel_id=1, source_target_pairs={{0,8},{8,0},{16,24},{24,16},{1,9},{9,1},{17,25},{25,17},{2,10},{10... | collective-permute-start | bytes 2359304 | tf_op jit(solution)/shard_map/ppermute | solution.py:1506
  261.1 56.7 %collective-permute-start.28 = (bf16[3,1,128,1024]{3,2,0,1:T(8,128)(2,1)S(1)}, bf16[3,1,128,1024]{3,2,0,1:T(8,128)(2,1)S(1)}, u32[]{:S(2)}, u32[]{:S(2)}) collective-permute-start(bf16[3,1,128,1024]{3,2,0,1:T(8,128)(2,1)S(1)} %pad_maximum_fusion.17), channel_id=1, source_target_pairs={{0,16},{8,24},{16,0},{24,8},{1,17},{9,25},{17,1},{25,9},{2,18},{10... | collective-permute-start | bytes 2359304 | tf_op jit(solution)/shard_map/ppermute | solution.py:1506
  262.6 55.2 %collective-permute-start.29 = (bf16[3,1,128,1024]{3,2,0,1:T(8,128)(2,1)S(1)}, bf16[3,1,128,1024]{3,2,0,1:T(8,128)(2,1)S(1)}, u32[]{:S(2)}, u32[]{:S(2)}) collective-permute-start(bf16[3,1,128,1024]{3,2,0,1:T(8,128)(2,1)S(1)} %pad_maximum_fusion.17), channel_id=1, source_target_pairs={{0,24},{8,16},{16,8},{24,0},{1,25},{9,17},{17,9},{25,1},{2,26},{10... | collective-permute-start | bytes 2359304 | tf_op jit(solution)/shard_map/ppermute | solution.py:1506
  263.9 53.8 %collective-permute-start.31 = (bf16[2,128,1024]{2,1,0:T(8,128)(2,1)S(1)}, bf16[2,128,1024]{2,1,0:T(8,128)(2,1)S(1)}, u32[]{:S(2)}, u32[]{:S(2)}) collective-permute-start(bf16[2,128,1024]{2,1,0:T(8,128)(2,1)S(1)} %fusion.18), channel_id=1, source_target_pairs={{0,4},{2,6},{4,0},{6,2},{1,5},{3,7},{5,1},{7,3},{8,12},{10,14},{12... | collective-permute-start | bytes 1572872 | tf_op jit(solution)/shard_map/ppermute | solution.py:1502
  266.7 51.0 %collective-permute-start.32 = (bf16[2,128,1024]{2,1,0:T(8,128)(2,1)S(1)}, bf16[2,128,1024]{2,1,0:T(8,128)(2,1)S(1)}, u32[]{:S(2)}, u32[]{:S(2)}) collective-permute-start(bf16[2,128,1024]{2,1,0:T(8,128)(2,1)S(1)} %fusion.18), channel_id=1, source_target_pairs={{0,6},{2,4},{4,2},{6,0},{1,7},{3,5},{5,3},{7,1},{8,14},{10,12},{12... | collective-permute-start | bytes 1572872 | tf_op jit(solution)/shard_map/ppermute | solution.py:1502
  320.8 437.5 %reduce-scatter.10.cloned.1.call-start = ((), (), s32[]{:S(2)}) async-start(), calls=%async_computation.6 | async-start | bytes 10485760
  355.1 51.3 %collective-permute-start.35 = (bf16[1024,1024]{1,0:T(8,128)(2,1)}, bf16[1024,1024]{1,0:T(8,128)(2,1)}, u32[]{:S(2)}, u32[]{:S(2)}) collective-permute-start(bf16[1024,1024]{1,0:T(8,128)(2,1)} %get-tuple-element.376.own), channel_id=1, source_target_pairs={{0,2},{1,3},{4,6},{5,7},{8,10},{9,11},{12,14},{13,15},{16,18},{17,... | collective-permute-start | bytes 6291464 | tf_op jit(solution)/shard_map/ppermute | solution.py:1578
  360.1 46.3 %collective-permute-start.36 = (bf16[1024,1024]{1,0:T(8,128)(2,1)}, bf16[1024,1024]{1,0:T(8,128)(2,1)}, u32[]{:S(2)}, u32[]{:S(2)}) collective-permute-start(bf16[1024,1024]{1,0:T(8,128)(2,1)} %get-tuple-element.376.own), channel_id=1, source_target_pairs={{0,1},{1,0},{2,3},{3,2},{4,5},{5,4},{6,7},{7,6},{8,9},{9,8},{10,11... | collective-permute-start | bytes 6291464 | tf_op jit(solution)/shard_map/ppermute | solution.py:1498
  518.4 36.3 %collective-permute-start.40 = (bf16[1024,1024]{1,0:T(8,128)(2,1)}, bf16[1024,1024]{1,0:T(8,128)(2,1)S(1)}, u32[]{:S(2)}, u32[]{:S(2)}) collective-permute-start(bf16[1024,1024]{1,0:T(8,128)(2,1)} %get-tuple-element.390.g_own), channel_id=1, source_target_pairs={{0,1},{1,0},{2,3},{3,2},{4,5},{5,4},{6,7},{7,6},{8,9},{9,8},{10,11... | collective-permute-start | bytes 6291464 | tf_op jit(solution)/shard_map/ppermute | solution.py:1498
  522.0 56.2 %collective-permute-start.41 = (bf16[1024,1024]{1,0:T(8,128)(2,1)}, bf16[1024,1024]{1,0:T(8,128)(2,1)S(1)}, u32[]{:S(2)}, u32[]{:S(2)}) collective-permute-start(bf16[1024,1024]{1,0:T(8,128)(2,1)} %get-tuple-element.390.g_own), channel_id=1, source_target_pairs={{2,0},{3,1},{6,4},{7,5},{10,8},{11,9},{14,12},{15,13},{18,16},{19,... | collective-permute-start | bytes 6291464 | tf_op jit(solution)/shard_map/ppermute | solution.py:1578
  578.2 69.1 %collective-permute-start.43 = (bf16[4,4,128,1024]{3,2,1,0:T(8,128)(2,1)}, bf16[4,4,128,1024]{3,2,1,0:T(8,128)(2,1)}, u32[]{:S(2)}, u32[]{:S(2)}) collective-permute-start(bf16[4,4,128,1024]{3,2,1,0:T(8,128)(2,1)} %get-tuple-element.416), channel_id=1, source_target_pairs={{0,1},{1,0},{2,3},{3,2},{4,5},{5,4},{6,7},{7,6},{8,9},{9,8},{10,11... | collective-permute-start | bytes 12582920 | tf_op jit(solution)/shard_map/ppermute | solution.py:1498
  578.2 69.1 %collective-permute-start.44 = (bf16[4,4,128,1024]{3,2,1,0:T(8,128)(2,1)}, bf16[4,4,128,1024]{3,2,1,0:T(8,128)(2,1)}, u32[]{:S(2)}, u32[]{:S(2)}) collective-permute-start(bf16[4,4,128,1024]{3,2,1,0:T(8,128)(2,1)} %get-tuple-element.417), channel_id=1, source_target_pairs={{0,1},{1,0},{2,3},{3,2},{4,5},{5,4},{6,7},{7,6},{8,9},{9,8},{10,11... | collective-permute-start | bytes 12582920 | tf_op jit(solution)/shard_map/ppermute | solution.py:1498
  590.4 55.8 %collective-permute-start.45 = (bf16[4,4,32,1024]{3,2,1,0:T(8,128)(2,1)S(1)}, bf16[4,4,32,1024]{3,2,1,0:T(8,128)(2,1)S(1)}, u32[]{:S(2)}, u32[]{:S(2)}) collective-permute-start(bf16[4,4,32,1024]{3,2,1,0:T(8,128)(2,1)S(1)} %bitcast.272), channel_id=1, source_target_pairs={{0,1},{1,0},{2,3},{3,2},{4,5},{5,4},{6,7},{7,6},{8,9},{9,8},{10,11... | collective-permute-start | bytes 3145736 | tf_op jit(solution)/shard_map/ppermute | solution.py:1498
  661.5 164.3 %reduce-scatter.12.cloned.1.call-start = ((), (), s32[]{:S(2)}) async-start(), calls=%async_computation.7 | async-start | bytes 5242880
  758.3 163.2 %reduce-scatter.8.cloned.1.call-start = ((), (), s32[]{:S(2)}) async-start(), calls=%async_computation.3 | async-start | bytes 3932160 | tf_op jit(solution)/shard_map/reduce_scatter | solution.py:1551
  758.4 46.7 %collective-permute-start.48 = (bf16[1024,1024]{1,0:T(8,128)(2,1)}, bf16[1024,1024]{1,0:T(8,128)(2,1)}, u32[]{:S(2)}, u32[]{:S(2)}) collective-permute-start(bf16[1024,1024]{1,0:T(8,128)(2,1)} %get-tuple-element.461.g_own), channel_id=1, source_target_pairs={{0,1},{1,0},{2,3},{3,2},{4,5},{5,4},{6,7},{7,6},{8,9},{9,8},{10,11... | collective-permute-start | bytes 6291464 | tf_op jit(solution)/shard_map/ppermute | solution.py:1498
  758.4 50.2 %collective-permute-start.49 = (bf16[1024,1024]{1,0:T(8,128)(2,1)}, bf16[1024,1024]{1,0:T(8,128)(2,1)}, u32[]{:S(2)}, u32[]{:S(2)}) collective-permute-start(bf16[1024,1024]{1,0:T(8,128)(2,1)} %get-tuple-element.461.g_own), channel_id=1, source_target_pairs={{2,0},{3,1},{6,4},{7,5},{10,8},{11,9},{14,12},{15,13},{18,16},{19,... | collective-permute-start | bytes 6291464 | tf_op jit(solution)/shard_map/ppermute | solution.py:1578
  853.5 269.9 %all-gather.7.cloned.1.call-start = ((), (), s32[]{:S(2)}) async-start(), calls=%async_computation.5 | async-start | bytes 3932160 | tf_op jit(solution)/shard_map/all_gather | solution.py:1555
  853.5 59.0 %collective-permute-start.57 = (bf16[2,4,144,1024]{3,2,1,0:T(8,128)(2,1)}, bf16[2,4,144,1024]{3,2,1,0:T(8,128)(2,1)}, u32[]{:S(2)}, u32[]{:S(2)}) collective-permute-start(bf16[2,4,144,1024]{3,2,1,0:T(8,128)(2,1)} %copy-done.75), channel_id=1, source_target_pairs={{0,8},{8,0},{16,24},{24,16},{1,9},{9,1},{17,25},{25,17},{2,10},{10... | collective-permute-start | bytes 7077896 | tf_op jit(solution)/shard_map/ppermute | solution.py:1506
  855.0 57.6 %collective-permute-start.58 = (bf16[2,4,144,1024]{3,2,1,0:T(8,128)(2,1)}, bf16[2,4,144,1024]{3,2,1,0:T(8,128)(2,1)}, u32[]{:S(2)}, u32[]{:S(2)}) collective-permute-start(bf16[2,4,144,1024]{3,2,1,0:T(8,128)(2,1)} %copy-done.74), channel_id=1, source_target_pairs={{0,16},{8,24},{16,0},{24,8},{1,17},{9,25},{17,1},{25,9},{2,18},{10... | collective-permute-start | bytes 7077896 | tf_op jit(solution)/shard_map/ppermute | solution.py:1506
  855.6 56.9 %collective-permute-start.56 = (f32[85,1024]{1,0:T(8,128)S(1)}, f32[85,1024]{1,0:T(8,128)S(1)}, u32[]{:S(2)}, u32[]{:S(2)}) collective-permute-start(f32[85,1024]{1,0:T(8,128)S(1)} %copy-done.117), channel_id=1, source_target_pairs={{0,4},{2,6},{4,0},{6,2},{1,5},{3,7},{5,1},{7,3},{8,12},{10,14},{12... | collective-permute-start | bytes 1044488 | tf_op jit(solution)/shard_map/ppermute | solution.py:1502
  923.5 35.3 %collective-permute-start.62 = (bf16[4,144,1024]{2,1,0:T(8,128)(2,1)S(1)}, bf16[4,144,1024]{2,1,0:T(8,128)(2,1)S(1)}, u32[]{:S(2)}, u32[]{:S(2)}) collective-permute-start(bf16[4,144,1024]{2,1,0:T(8,128)(2,1)S(1)} %fusion.3), channel_id=1, source_target_pairs={{0,8},{8,0},{16,24},{24,16},{1,9},{9,1},{17,25},{25,17},{2,10},{10... | collective-permute-start | bytes 3538952 | tf_op jit(solution)/shard_map/ppermute | solution.py:1506
  926.7 32.1 %collective-permute-start.61 = (bf16[4,144,1024]{2,1,0:T(8,128)(2,1)S(1)}, bf16[4,144,1024]{2,1,0:T(8,128)(2,1)S(1)}, u32[]{:S(2)}, u32[]{:S(2)}) collective-permute-start(bf16[4,144,1024]{2,1,0:T(8,128)(2,1)S(1)} %fusion.2), channel_id=1, source_target_pairs={{0,16},{8,24},{16,0},{24,8},{1,17},{9,25},{17,1},{25,9},{2,18},{10... | collective-permute-start | bytes 3538952 | tf_op jit(solution)/shard_map/ppermute | solution.py:1506
  996.5 46.6 %collective-permute-start.65 = (bf16[4,96,1024]{2,1,0:T(8,128)(2,1)}, bf16[4,96,1024]{2,1,0:T(8,128)(2,1)}, u32[]{:S(2)}, u32[]{:S(2)}) collective-permute-start(bf16[4,96,1024]{2,1,0:T(8,128)(2,1)} %get-tuple-element.557), channel_id=1, source_target_pairs={{0,8},{8,0},{16,24},{24,16},{1,9},{9,1},{17,25},{25,17},{2,10},{10... | collective-permute-start | bytes 2359304 | tf_op jit(solution)/shard_map/ppermute | solution.py:1506
  997.5 45.6 %collective-permute-start.66 = (bf16[4,96,1024]{2,1,0:T(8,128)(2,1)}, bf16[4,96,1024]{2,1,0:T(8,128)(2,1)}, u32[]{:S(2)}, u32[]{:S(2)}) collective-permute-start(bf16[4,96,1024]{2,1,0:T(8,128)(2,1)} %get-tuple-element.558), channel_id=1, source_target_pairs={{0,16},{8,24},{16,0},{24,8},{1,17},{9,25},{17,1},{25,9},{2,18},{10... | collective-permute-start | bytes 2359304 | tf_op jit(solution)/shard_map/ppermute | solution.py:1506
  998.7 44.4 %collective-permute-start.67 = (bf16[4,96,1024]{2,1,0:T(8,128)(2,1)}, bf16[4,96,1024]{2,1,0:T(8,128)(2,1)}, u32[]{:S(2)}, u32[]{:S(2)}) collective-permute-start(bf16[4,96,1024]{2,1,0:T(8,128)(2,1)} %get-tuple-element.559), channel_id=1, source_target_pairs={{0,24},{8,16},{16,8},{24,0},{1,25},{9,17},{17,9},{25,1},{2,26},{10... | collective-permute-start | bytes 2359304 | tf_op jit(solution)/shard_map/ppermute | solution.py:1506
  1002.2 40.8 %collective-permute-start.68 = (bf16[288,1024]{1,0:T(8,128)(2,1)S(1)}, bf16[288,1024]{1,0:T(8,128)(2,1)S(1)}, u32[]{:S(2)}, u32[]{:S(2)}) collective-permute-start(bf16[288,1024]{1,0:T(8,128)(2,1)S(1)} %get-tuple-element.655), channel_id=1, source_target_pairs={{0,4},{2,6},{4,0},{6,2},{1,5},{3,7},{5,1},{7,3},{8,12},{10,14},{12... | collective-permute-start | bytes 1769480 | tf_op jit(solution)/shard_map/ppermute | solution.py:1502
  1023.1 29.1 %collective-permute-start.70 = (bf16[288,1024]{1,0:T(8,128)(2,1)}, bf16[288,1024]{1,0:T(8,128)(2,1)S(1)}, u32[]{:S(2)}, u32[]{:S(2)}) collective-permute-start(bf16[288,1024]{1,0:T(8,128)(2,1)} %get-tuple-element.654), channel_id=1, source_target_pairs={{0,6},{2,4},{4,2},{6,0},{1,7},{3,5},{5,3},{7,1},{8,14},{10,12},{12... | collective-permute-start | bytes 1769480 | tf_op jit(solution)/shard_map/ppermute | solution.py:1502
  1075.9 46.4 %collective-permute-start.78 = (bf16[384,1024]{1,0:T(8,128)(2,1)S(1)}, bf16[384,1024]{1,0:T(8,128)(2,1)S(1)}, u32[]{:S(2)}, u32[]{:S(2)}) collective-permute-start(bf16[384,1024]{1,0:T(8,128)(2,1)S(1)} %pad_maximum_fusion.18.zero), channel_id=1, source_target_pairs={{0,8},{8,0},{16,24},{24,16},{1,9},{9,1},{17,25},{25,17},{2,10},{10... | collective-permute-start | bytes 2359304 | tf_op jit(solution)/shard_map/ppermute | solution.py:1506
  1077.0 45.3 %collective-permute-start.79 = (bf16[384,1024]{1,0:T(8,128)(2,1)S(1)}, bf16[384,1024]{1,0:T(8,128)(2,1)S(1)}, u32[]{:S(2)}, u32[]{:S(2)}) collective-permute-start(bf16[384,1024]{1,0:T(8,128)(2,1)S(1)} %pad_maximum_fusion.18.zero), channel_id=1, source_target_pairs={{0,16},{8,24},{16,0},{24,8},{1,17},{9,25},{17,1},{25,9},{2,18},{10... | collective-permute-start | bytes 2359304 | tf_op jit(solution)/shard_map/ppermute | solution.py:1506
  1078.1 44.2 %collective-permute-start.80 = (bf16[384,1024]{1,0:T(8,128)(2,1)S(1)}, bf16[384,1024]{1,0:T(8,128)(2,1)S(1)}, u32[]{:S(2)}, u32[]{:S(2)}) collective-permute-start(bf16[384,1024]{1,0:T(8,128)(2,1)S(1)} %pad_maximum_fusion.18.zero), channel_id=1, source_target_pairs={{0,24},{8,16},{16,8},{24,0},{1,25},{9,17},{17,9},{25,1},{2,26},{10... | collective-permute-start | bytes 2359304 | tf_op jit(solution)/shard_map/ppermute | solution.py:1506
  1084.3 36.2 %collective-permute-start.81 = (f32[85,1024]{1,0:T(8,128)S(1)}, f32[85,1024]{1,0:T(8,128)S(1)}, u32[]{:S(2)}, u32[]{:S(2)}) collective-permute-start(f32[85,1024]{1,0:T(8,128)S(1)} %add.339), channel_id=1, source_target_pairs={{0,16},{8,24},{16,0},{24,8},{1,17},{9,25},{17,1},{25,9},{2,18},{10... | collective-permute-start | bytes 1044488 | tf_op jit(solution)/shard_map/ppermute | solution.py:1506
  (199 other events, 3216.2 us)
Sparse Core Ops, SparseCore 0:
  320.9 71.8 all-gather.4
  661.6 96.6 reduce-scatter.9
  762.1 52.6 reduce-scatter.11
  853.6 67.9 reduce-scatter.7
  960.5 55.3 all-gather.6
